TPU v7x, 32 devices: a whole 2x2x4 slice. The times are simulated.
32 devices in a mesh: ctx: 8 (over y, x, core), ch: 4 (over z).
Axes of the slice: x: 2, y: 2, z: 4, core: 2. Of those that a mesh axis runs over, the one named last changes fastest.
Arguments:
- gate_query: bfloat16 [2048, 8192], P('ctx', 'ch'), may hold values from -6 to 6
- gate_key: bfloat16 [2048, 8192], P('ctx', 'ch'), may hold values from -6 to 6
- value_in: bfloat16 [2048, 8192], P('ctx', 'ch'), may hold values from -6 to 6
- mr_filter: bfloat16 [128, 512], P(None, 'ch'), may hold values from -0.5 to 0.5
- pole_rates: float32 [16, 512], P(None, 'ch'), may hold values from 2.4414063e-05 to 0.05
- residues: float32 [16, 512], P(None, 'ch'), may hold values from -3 to 3
- skip_gain: float32 [8192], P('ch'), may hold values from -4 to 4
- offsets: int32 [65], replicated, may hold values from 0 to 2048, as said below
- owner_docs: int32 [32], replicated, may hold values from 0 to 63, as said below
Outputs:
- output: bfloat16 [2048, 8192], P('ctx', 'ch')
- doc_states: float32 [32, 16, 8192], P(('ctx', 'ch'))
Inputs may be any that keep to these rules, and one draw needn't show every extreme that they name: offsets[0] = 0 and offsets[64] = 2048, strictly increasing; document d holds tokens offsets[d] to offsets[d + 1] - 1. The last tokens of at most 16 documents lie among the 256 tokens of one index of ctx, and some index holds exactly 16. `owner_docs`: for some base b, slot r * 4 + k (k < 4) holds document (b + k * 8 + r) mod 64.
All inputs are finite; a program needn't handle non-finite values.
Results may differ from a plain program's by a relative error of at most 0.0049.
Values may be sent and summed in bfloat16 or wider, within the bound.
No kernel may reach another device: no remote copies, remote signals or barrier semaphores. Data moves between devices by JAX's collectives and lax.ppermute only.
A program may use at most 320 MiB of HBM per device.

v0:
```python
import functools

import jax
import jax.numpy as jnp
from jax import lax
from jax.experimental import pallas as pl
from jax.experimental.pallas import tpu as pltpu
from jax.sharding import PartitionSpec as P

TAPS = 128
ENDS = 16
LANES = 128
BLOCK = 512
CHUNK = 16
F32 = jnp.float32
BF16 = jnp.bfloat16

SMEM = pl.BlockSpec(memory_space=pltpu.SMEM)


def params(grid_dims, mebibytes):
    return pltpu.CompilerParams(
        dimension_semantics=("arbitrary",) * grid_dims, vmem_limit_bytes=mebibytes * 1024 * 1024
    )


def iota(shape, dim):
    return lax.broadcasted_iota(jnp.int32, shape, dim)


def dot(a, b):
    return lax.dot_general(a, b, (((1,), (0,)), ((), ())), preferred_element_type=F32)


def dot_t(a, b):
    return lax.dot_general(a, b, (((0,), (0,)), ((), ())), preferred_element_type=F32)


def spread(x, first_group, size, lanes):
    groups = x.shape[1]
    pick = (iota((groups, lanes), 0) == first_group + iota((groups, lanes), 1) // size).astype(F32)
    pick = pick.astype(BF16)
    high = x.astype(BF16)
    rest = x - high.astype(F32)
    mid = rest.astype(BF16)
    low = (rest - mid.astype(F32)).astype(BF16)
    return dot(high, pick) + dot(mid, pick) + dot(low, pick)


def gain(rates):
    x = 2.0 * rates
    tail = 1.0 - x / 9.0
    for k in range(8, 1, -1):
        tail = 1.0 - x * tail * (1.0 / k)
    return jnp.sqrt(x * tail)


def circulant(row):
    return pltpu.roll(
        jnp.broadcast_to(row, (TAPS, TAPS)), 0, 1, stride=1, stride_axis=0
    ).astype(BF16)


def doc_at(offsets, position):
    docs = offsets.shape[0] - 1
    low, high = jnp.int32(0), jnp.int32(docs)
    for _ in range(docs.bit_length()):
        middle = (low + high) // 2
        left = offsets[middle] <= position
        low, high = jnp.where(left, middle, low), jnp.where(left, high, middle)
    return low


def filtered(blocks, masks, earlier, current, window, key):
    lane_group = iota((TAPS, LANES), 1) // (LANES // len(blocks))
    total = jnp.zeros((TAPS, LANES), F32)
    for g, c in enumerate(blocks):
        y = dot(jnp.concatenate([c * masks[earlier], c * masks[current]], axis=1), window)
        total = jnp.where(lane_group == g, y, total)
    return (key.astype(F32) * total).astype(BF16)


def prepare_kernel(
    cap,
    peers,
    size,
    offsets,
    owners,
    place,
    filt,
    rates,
    resid,
    rates_out,
    gains_out,
    rows_out,
    masks_out,
    taps_out,
    keep,
    last,
):
    poles, groups = rates.shape
    width = rates_out.shape[1]
    length = 2 * TAPS
    docs = offsets.shape[0] - 1
    chosen = owners.shape[0]
    begin = place[0] * length
    d0 = doc_at(offsets, begin)

    def clear(t, carry):
        for u in range(8):
            keep[t * 8 + u] = jnp.float32(1.0)
        return carry

    lax.fori_loop(0, length // 8, clear, 0)
    for row in range(peers * cap):
        last[row] = 0

    def mark(k, carry):
        doc = d0 + k
        order = lax.rem(doc - owners[0] + docs, docs)
        start = offsets[jnp.minimum(doc, docs)] - begin
        end = offsets[jnp.minimum(doc + 1, docs)] - 1 - begin

        @pl.when((doc < docs) & (start >= 0) & (start < length))
        def opens():
            keep[start] = jnp.float32(0.0)

        @pl.when((doc < docs) & (end < length) & (order < chosen))
        def closes():
            last[lax.rem(order, peers) * cap + lax.rem(order // peers, cap)] = end

        return carry

    lax.fori_loop(0, ENDS + 1, mark, 0)

    spot = begin + iota((length, LANES), 0)
    starts = jnp.broadcast_to(offsets[d0], (length, LANES))
    for k in range(1, ENDS + 1):
        off = offsets[jnp.minimum(d0 + k, docs)]
        starts = jnp.where(spot >= off, off, starts)
    i, j = iota((TAPS, TAPS), 0), iota((TAPS, TAPS), 1)
    s0, s1 = starts[:TAPS], starts[TAPS:]
    cross = s1 <= begin + j
    for index, mask in enumerate(
        (
            (j > i) & (s0 <= begin - TAPS + j),
            (j <= i) & (s0 <= begin + j),
            (j > i) & cross,
            (j <= i) & (s1 <= begin + TAPS + j),
            (j <= i) & cross,
        )
    ):
        masks_out[index] = mask.astype(F32).astype(BF16)
    turn = (i == (TAPS - j) % TAPS).astype(F32).astype(BF16)
    rows_out[...] = dot_t(filt[...], turn)
    lag = iota((TAPS, groups), 0).astype(F32)
    gains = gain(rates[...])
    weight = resid[...] * gains
    near = jnp.zeros((TAPS, groups), F32)
    far = jnp.zeros((TAPS, groups), F32)
    for n in range(poles):
        term = weight[n : n + 1] * jnp.exp(-rates[n : n + 1] * lag)
        near = near + term
        far = far + term * jnp.exp(-rates[n : n + 1] * float(TAPS))
    taps_out[0] = dot_t(near.astype(BF16), turn)
    taps_out[1] = dot_t(far.astype(BF16), turn)
    for tile in range(width // LANES):
        at = pl.ds(tile * LANES, LANES)
        wide = spread(rates[...], tile * (LANES // size), size, LANES)
        rates_out[:, at] = wide
        gains_out[:, at] = gain(wide)


def states_kernel(
    cap,
    size,
    place,
    keep,
    last,
    halo,
    value,
    key,
    rows,
    masks,
    rates,
    gains,
    mixed_out,
    *rest,
):
    ends_out, (wide, history) = rest[:-2], rest[-2:]
    poles, width = rates.shape
    length, block = value.shape
    peers = len(ends_out)
    step = pl.program_id(0)
    per_tile = LANES // size

    for tile in range(block // LANES):
        at = slice(tile * LANES, (tile + 1) * LANES)
        spot = pl.ds(pl.multiple_of(step * block + tile * LANES, LANES), LANES)
        x = value[:, at]
        window = jnp.concatenate([halo[:, at], x[:TAPS]], axis=0)
        blocks = [
            circulant(rows[tile * per_tile + g : tile * per_tile + g + 1]) for g in range(per_tile)
        ]
        mixed0 = filtered(blocks, masks, 0, 1, window, key[:TAPS, at])
        mixed1 = filtered(blocks, masks, 2, 3, x, key[TAPS:, at])
        mixed_out[:TAPS, at] = mixed0
        mixed_out[TAPS:, at] = mixed1
        wide[:TAPS, spot] = mixed0.astype(F32)
        wide[TAPS:, spot] = mixed1.astype(F32)

    @pl.when(step == pl.num_programs(0) - 1)
    def run():
        for first in range(0, width, block):
            lanes = slice(first, first + block)
            fade = jnp.exp(-rates[:, lanes])

            def some(c, state):
                base = pl.multiple_of(c * CHUNK, CHUNK)
                for t in range(CHUNK):
                    state = (fade * keep[base + t]) * state + wide[pl.ds(base + t, 1), lanes]
                    history[base + t] = state
                return state

            state = lax.fori_loop(0, length // CHUNK, some, jnp.zeros((poles, block), F32))
            scale = gains[:, lanes]
            through = (state * scale).astype(BF16)
            for d in range(peers):
                peer = lax.rem(place[0] + d, peers)
                for i in range(cap):
                    end = history[last[peer * cap + i]]
                    ends_out[d][i, :, lanes] = (end * scale).astype(BF16)
                ends_out[d][cap, :, lanes] = through


def local_kernel(
    size, offsets, place, mixed, masks, taps, skip, rates, resid, local_out, weight_out, limit
):
    length, block = mixed.shape
    begin = place[0] * length
    step = pl.program_id(0)
    per_tile = LANES // size

    @pl.when(step == 0)
    def prepare():
        doc = doc_at(offsets, begin)
        limit[0] = jnp.where(offsets[doc] < begin, offsets[doc + 1] - begin, 0)

    t = iota((length, LANES), 0)
    lane_group = iota((TAPS, LANES), 1) // size
    for tile in range(block // LANES):
        at = slice(tile * LANES, (tile + 1) * LANES)
        x = mixed[:, at]
        acc0 = jnp.zeros((TAPS, LANES), F32)
        acc1 = jnp.zeros((TAPS, LANES), F32)
        for g in range(per_tile):
            row = tile * per_tile + g
            a, b = circulant(taps[0, row : row + 1]), circulant(taps[1, row : row + 1])
            y0 = dot(a * masks[1], x[:TAPS])
            y1 = dot(jnp.concatenate([a * masks[2] + b * masks[4], a * masks[3]], axis=1), x)
            acc0 = jnp.where(lane_group == g, y0, acc0)
            acc1 = jnp.where(lane_group == g, y1, acc1)
        local_out[:, at] = jnp.concatenate([acc0, acc1], axis=0) + skip[:, at] * x.astype(F32)
        weight = jnp.exp(-rates[:, at] * (t + 1).astype(F32)) * resid[:, at]
        weight = jnp.where(t < limit[0], weight, 0.0)
        weight_out[:, at] = weight.astype(BF16)


def slots_kernel(length, lines, peers, offsets, owners, place, line, *rest):
    got, (rates, after, entering_out) = rest[:peers], rest[peers : peers + 3]
    slot_outs = rest[peers + 3 : peers + 3 + lines]
    through, mine, sems = rest[peers + 3 + lines :]
    cap = got[0].shape[0] - 1
    per_line = slot_outs[0].shape[0]
    me = place[0]
    arriving = []
    for d in range(peers):
        source = lax.rem(me - d + peers, peers)
        arriving.append(pltpu.make_async_copy(got[d].at[cap], through.at[source], sems.at[d]))
        arriving[-1].start()
    spans = []
    for d in range(lines):
        for q in range(per_line):
            k = lax.rem(line[0] + d, lines) * per_line + q
            doc = owners[me * (lines * per_line) + k]
            start, end = offsets[doc], offsets[doc + 1] - 1
            spot = d * per_line + q
            behind = lax.rem(me - end // length + peers, peers)
            for e in range(peers):

                @pl.when(behind == e)
                def fetch(e=e, k=k, spot=spot):
                    pltpu.make_async_copy(
                        got[e].at[lax.rem(k, cap)], mine.at[spot], sems.at[peers + spot]
                    ).start()

            spans.append((start, end))
    p = rates[...]
    fade = jnp.exp(-p * float(length))

    def entering(first, stop):
        def hop(c, state):
            return fade * state + through[c].astype(F32)

        return lax.fori_loop(first, stop, hop, jnp.zeros(p.shape, F32))

    my_start = offsets[doc_at(offsets, me * length)]
    for copy in arriving:
        copy.wait()
    for spot, (start, end) in enumerate(spans):
        source = end // length
        link = jnp.exp(-p * (end - source * length + 1).astype(F32))
        extra = link * entering(start // length, source)
        pltpu.make_async_copy(got[0].at[0], mine.at[spot], sems.at[peers + spot]).wait()
        state = mine[spot].astype(F32) + extra
        slot_outs[spot // per_line][spot % per_line] = state.astype(BF16)
    entering_out[...] = entering(my_start // length, me)


def output_kernel(size, query, local, entering, weight, out):
    poles, width = entering.shape
    tile = 2 * LANES
    kept = iota((tile, tile), 0) // poles == iota((tile, tile), 1) // size
    kept = kept.astype(F32).astype(BF16)
    for first in range(0, width, tile):
        at = slice(first, first + tile)
        spread_out = jnp.concatenate([entering[:, at].astype(BF16)] * (tile // size), axis=0) * kept
        fix = dot(weight[:, at], spread_out)
        out[:, at] = (query[:, at].astype(F32) * (local[:, at] + fix)).astype(BF16)


def widen_kernel(line, *refs):
    parts, out = refs[:-1], refs[-1]
    width = parts[0].shape[2]
    for d, part in enumerate(parts):
        source = lax.rem(line[0] - d + len(parts), len(parts))
        out[:, :, pl.ds(pl.multiple_of(source * width, width), width)] = part[...].astype(F32)


def per_device(query, key, value, filt, rates, resid, skip, offsets, owners):
    length, width = value.shape
    poles, groups = rates.shape
    size = width // groups
    peers, lines = lax.axis_size("ctx"), lax.axis_size("ch")
    slots = owners.shape[0] // peers
    cap = -(-ENDS // peers)
    line = lax.axis_index("ch").astype(jnp.int32).reshape(1)
    place = lax.axis_index("ctx").astype(jnp.int32).reshape(1)
    rates_flat = rates.T.reshape(1, groups * poles)
    resid_flat = resid.T.reshape(1, groups * poles)

    halo = lax.ppermute(
        value[length - TAPS :], "ctx", [(i, i + 1) for i in range(peers - 1)]
    )

    def whole(shape):
        return pl.BlockSpec(shape, lambda i: (0,) * len(shape))

    block = min(width, BLOCK)

    def lanes(height):
        return pl.BlockSpec((height, block), lambda i: (0, i))

    vmem = pl.BlockSpec(memory_space=pltpu.VMEM)
    hbm = pl.BlockSpec(memory_space=pl.ANY)
    rates_wide, gains_wide, rows, masks, taps, keep, last = pl.pallas_call(
        functools.partial(prepare_kernel, cap, peers, size),
        in_specs=[SMEM] * 3 + [vmem] * 3,
        out_specs=[vmem] * 5 + [SMEM] * 2,
        out_shape=[
            jax.ShapeDtypeStruct((poles, width), F32),
            jax.ShapeDtypeStruct((poles, width), F32),
            jax.ShapeDtypeStruct((groups, TAPS), F32),
            jax.ShapeDtypeStruct((5, TAPS, TAPS), BF16),
            jax.ShapeDtypeStruct((2, groups, TAPS), F32),
            jax.ShapeDtypeStruct((length,), F32),
            jax.ShapeDtypeStruct((peers * cap,), jnp.int32),
        ],
        compiler_params=params(0, 60),
        cost_estimate=pl.CostEstimate(flops=1 << 30, bytes_accessed=1 << 20, transcendentals=0),
        name="prepare",
    )(offsets, owners, place, filt, rates, resid)

    mixed, *ends = pl.pallas_call(
        functools.partial(states_kernel, cap, size),
        grid=(width // block,),
        in_specs=[
            SMEM,
            SMEM,
            SMEM,
            lanes(TAPS),
            lanes(length),
            lanes(length),
            pl.BlockSpec((block // size, TAPS), lambda i: (i, 0)),
            whole((5, TAPS, TAPS)),
            whole((poles, width)),
            whole((poles, width)),
        ],
        out_specs=[lanes(length)] + [whole((cap + 1, poles, width))] * peers,
        out_shape=[jax.ShapeDtypeStruct((length, width), BF16)]
        + [jax.ShapeDtypeStruct((cap + 1, poles, width), BF16)] * peers,
        scratch_shapes=[
            pltpu.VMEM((length, width), F32),
            pltpu.VMEM((length, poles, block), F32),
        ],
        compiler_params=params(1, 56),
        name="states",
    )(place, keep, last, halo, value, key, rows, masks, rates_wide, gains_wide)

    got = [ends[0]]
    for d in range(1, peers):
        route = [(i, (i + d) % peers) for i in range(peers)]
        got.append(lax.ppermute(ends[d], "ctx", route))

    local, weight = pl.pallas_call(
        functools.partial(local_kernel, size),
        grid=(width // block,),
        in_specs=[
            SMEM,
            SMEM,
            lanes(length),
            whole((5, TAPS, TAPS)),
            pl.BlockSpec((2, block // size, TAPS), lambda i: (0, i, 0)),
            lanes(1),
            lanes(1),
            lanes(1),
        ],
        out_specs=[lanes(length)] * 2,
        out_shape=[
            jax.ShapeDtypeStruct((length, width), F32),
            jax.ShapeDtypeStruct((length, width), BF16),
        ],
        scratch_shapes=[pltpu.SMEM((1,), jnp.int32)],
        compiler_params=params(1, 48),
        cost_estimate=pl.CostEstimate(
            flops=32 * length * length * width, bytes_accessed=6 * length * width, transcendentals=0
        ),
        name="local",
    )(offsets, place, mixed, masks, taps, skip.reshape(1, width), rates_flat, resid_flat)

    per_line = slots // lines
    entering, *picked = pl.pallas_call(
        functools.partial(slots_kernel, length, lines, peers),
        in_specs=[SMEM] * 4 + [hbm] * peers + [vmem, hbm],
        out_specs=[vmem] * (1 + lines),
        out_shape=[jax.ShapeDtypeStruct((poles, width), F32)]
        + [jax.ShapeDtypeStruct((per_line, poles, width), BF16)] * lines,
        scratch_shapes=[
            pltpu.VMEM((peers, poles, width), BF16),
            pltpu.VMEM((slots, poles, width), BF16),
            pltpu.SemaphoreType.DMA((peers + slots,)),
        ],
        compiler_params=params(0, 16),
        name="slots",
    )(offsets, owners, place, line, *got, rates_wide, local)

    arrived = [picked[0]]
    for d in range(1, lines):
        route = [(i, (i + d) % lines) for i in range(lines)]
        arrived.append(lax.ppermute(picked[d], "ch", route))

    output = pl.pallas_call(
        functools.partial(output_kernel, size),
        grid=(width // block,),
        in_specs=[lanes(length), lanes(length), lanes(poles), lanes(length)],
        out_specs=lanes(length),
        out_shape=jax.ShapeDtypeStruct((length, width), BF16),
        compiler_params=params(1, 60),
        cost_estimate=pl.CostEstimate(
            flops=3 * 512 * length * width, bytes_accessed=12 * length * width, transcendentals=0
        ),
        name="output",
    )(query, local, entering, weight)

    doc_states = pl.pallas_call(
        widen_kernel,
        in_specs=[SMEM] + [vmem] * lines,
        out_specs=vmem,
        out_shape=jax.ShapeDtypeStruct((per_line, poles, lines * width), F32),
        compiler_params=params(0, 16),
        name="widen",
    )(line, *arrived)
    return (output, doc_states)


def solution(mesh):
    placed = (
        P("ctx", "ch"),
        P("ctx", "ch"),
        P("ctx", "ch"),
        P(None, "ch"),
        P(None, "ch"),
        P(None, "ch"),
        P("ch"),
        P(),
        P(),
    )
    return jax.shard_map(
        per_device,
        mesh=mesh,
        in_specs=placed,
        out_specs=(P("ctx", "ch"), P(("ctx", "ch"), None, None)),
        check_vma=False,
    )
```

profile of v0, /device:TPU:0, one launch (start us, length us, event | category | flops | bytes accessed | tf_op | source)
XLA Modules:
  0.0 62.3 jit_solution(12864980137487352299)
XLA Ops:
  0.6 1.1 %slice.3 = bf16[128,2048]{1,0:T(8,128)(2,1)S(1)} slice(bf16[256,2048]{1,0:T(8,128)(2,1)} %value.1), slice={[128:256], [0:2048]} | slice | bytes 1048576 | tf_op jit(solution)/shard_map/slice | solution.py:353
  1.7 2.4 %collective-permute-start = (bf16[128,2048]{1,0:T(8,128)(2,1)S(1)}, bf16[128,2048]{1,0:T(8,128)(2,1)S(1)}, u32[]{:S(2)}, u32[]{:S(2)}) collective-permute-start(bf16[128,2048]{1,0:T(8,128)(2,1)S(1)} %slice.3), channel_id=1, source_target_pairs={{0,4},{4,8},{8,12},{12,16},{16,20},{20,24},{24,28},{1,5},{5,9},{9,... | collective-permute-start | bytes 1572872 | tf_op jit(solution)/shard_map/ppermute | solution.py:352
  4.1 3.3 %prepare.1 = (f32[16,2048]{1,0:T(8,128)}, f32[16,2048]{1,0:T(8,128)}, f32[128,128]{1,0:T(8,128)}, bf16[5,128,128]{2,1,0:T(8,128)(2,1)}, f32[2,128,128]{2,1,0:T(8,128)}, /*index=5*/f32[256]{0:T(256)}, s32[16]{0:T(128)}) custom-call(s32[65]{0:T(128)} %offsets.5, s32[32]{0:T(128)} %owners.3, s32[1]{0:T(128)} %bitcast.place, bf16[128,128]{1,0:T(8,128)(2,1)} %filt.1, ...), custom_call_target="tpu_custom_call" | custom-call | flops 1073741824 | bytes 1048576 | tf_op jit(solution)/shard_map/prepare/pallas_call | solution.py:366
  7.4 0.0 copy-start.12
  7.5 0.0 copy-start.13
  7.5 0.0 copy-start.4
  7.5 0.0 copy-start.6
  7.5 0.0 copy-start.9
  7.5 0.0 copy-start.10
  7.5 0.0 collective-permute-done.halo
  7.5 0.0 copy-start.11
  7.5 0.8 %copy-done.11 = bf16[128,2048]{1,0:T(8,128)(2,1)} copy-done((bf16[128,2048]{1,0:T(8,128)(2,1)}, bf16[128,2048]{1,0:T(8,128)(2,1)S(1)}, u32[]{:S(2)}) %copy-start.11) | copy-done | bytes 524312
  8.3 12.4 %states.1 = (bf16[256,2048]{1,0:T(8,128)(2,1)}, bf16[3,16,2048]{2,1,0:T(8,128)(2,1)}, bf16[3,16,2048]{2,1,0:T(8,128)(2,1)}, bf16[3,16,2048]{2,1,0:T(8,128)(2,1)}...) custom-call(s32[1]{0:T(128)} %bitcast.place, ...), custom_call_target="tpu_custom_call" | custom-call | tf_op jit(solution)/shard_map/states/pallas_call | solution.py:384
  20.7 5.3 %collective-permute-start.1 = (bf16[3,16,2048]{2,1,0:T(8,128)(2,1)}, bf16[3,16,2048]{2,1,0:T(8,128)(2,1)S(1)}, u32[]{:S(2)}, u32[]{:S(2)}) collective-permute-start(bf16[3,16,2048]{2,1,0:T(8,128)(2,1)} %get-tuple-element.35), channel_id=1, source_target_pairs={{0,4},{4,8},{8,12},{12,16},{16,20},{20,24},{24,28},{28,0},{1,5},{5... | collective-permute-start | bytes 589832 | tf_op jit(solution)/shard_map/ppermute | solution.py:413
  26.0 2.4 %collective-permute-start.2 = (bf16[3,16,2048]{2,1,0:T(8,128)(2,1)}, bf16[3,16,2048]{2,1,0:T(8,128)(2,1)S(1)}, u32[]{:S(2)}, u32[]{:S(2)}) collective-permute-start(bf16[3,16,2048]{2,1,0:T(8,128)(2,1)} %get-tuple-element.36), channel_id=1, source_target_pairs={{0,8},{4,12},{8,16},{12,20},{16,24},{20,28},{24,0},{28,4},{1,9},{5... | collective-permute-start | bytes 589832 | tf_op jit(solution)/shard_map/ppermute | solution.py:413
  28.4 0.1 copy.14
  28.5 0.1 reshape.22.resid
  28.6 0.1 copy.13
  28.7 0.1 reshape.21.rates
  28.8 2.4 %collective-permute-start.3 = (bf16[3,16,2048]{2,1,0:T(8,128)(2,1)}, bf16[3,16,2048]{2,1,0:T(8,128)(2,1)S(1)}, u32[]{:S(2)}, u32[]{:S(2)}) collective-permute-start(bf16[3,16,2048]{2,1,0:T(8,128)(2,1)} %get-tuple-element.37), channel_id=1, source_target_pairs={{0,12},{4,16},{8,20},{12,24},{16,28},{20,0},{24,4},{28,8},{1,13},{... | collective-permute-start | bytes 589832 | tf_op jit(solution)/shard_map/ppermute | solution.py:413
  31.2 0.5 collective-permute-start.4
  31.8 0.7 %collective-permute-start.5 = (bf16[3,16,2048]{2,1,0:T(8,128)(2,1)}, bf16[3,16,2048]{2,1,0:T(8,128)(2,1)S(1)}, u32[]{:S(2)}, u32[]{:S(2)}) collective-permute-start(bf16[3,16,2048]{2,1,0:T(8,128)(2,1)} %get-tuple-element.39), channel_id=1, source_target_pairs={{0,20},{4,24},{8,28},{12,0},{16,4},{20,8},{24,12},{28,16},{1,21},{... | collective-permute-start | bytes 589832 | tf_op jit(solution)/shard_map/ppermute | solution.py:413
  32.5 0.0 collective-permute-done.1.rest_1_
  32.5 3.7 %collective-permute-start.6 = (bf16[3,16,2048]{2,1,0:T(8,128)(2,1)}, bf16[3,16,2048]{2,1,0:T(8,128)(2,1)S(1)}, u32[]{:S(2)}, u32[]{:S(2)}) collective-permute-start(bf16[3,16,2048]{2,1,0:T(8,128)(2,1)} %get-tuple-element.40), channel_id=1, source_target_pairs={{0,24},{4,28},{8,0},{12,4},{16,8},{20,12},{24,16},{28,20},{1,25},{... | collective-permute-start | bytes 589832 | tf_op jit(solution)/shard_map/ppermute | solution.py:413
  36.2 0.0 collective-permute-done.2.rest_2_
  36.2 3.9 %collective-permute-start.7 = (bf16[3,16,2048]{2,1,0:T(8,128)(2,1)}, bf16[3,16,2048]{2,1,0:T(8,128)(2,1)S(1)}, u32[]{:S(2)}, u32[]{:S(2)}) collective-permute-start(bf16[3,16,2048]{2,1,0:T(8,128)(2,1)} %get-tuple-element.41), channel_id=1, source_target_pairs={{0,28},{4,0},{8,4},{12,8},{16,12},{20,16},{24,20},{28,24},{1,29},{... | collective-permute-start | bytes 589832 | tf_op jit(solution)/shard_map/ppermute | solution.py:413
  40.1 0.0 copy-done.4
  40.1 0.0 copy-start.8
  40.1 1.2 %copy-done.8 = bf16[256,2048]{1,0:T(8,128)(2,1)S(1)} copy-done((bf16[256,2048]{1,0:T(8,128)(2,1)S(1)}, bf16[256,2048]{1,0:T(8,128)(2,1)}, u32[]{:S(2)}) %copy-start.8) | copy-done | bytes 1048600
  41.3 6.1 %local.1 = (f32[256,2048]{1,0:T(8,128)S(1)}, bf16[256,2048]{1,0:T(8,128)(2,1)S(1)}) custom-call(s32[65]{0:T(128)S(1)} %copy-done.6, s32[1]{0:T(128)} %bitcast.place, bf16[256,2048]{1,0:T(8,128)(2,1)S(1)} %copy-done.8, bf16[5,128,128]{2,1,0:T(8,128)(2,1)S(1)} %copy-done.4, f32[2,128,128]{2,1,0:T(8,128)S(1)} %copy-done.10, f32[1,2048]{1,0:T(1,128)S(1)} %bitcast.5, ...), custom_call_target="tpu_custom_call" | custom-call | flops 4294967296 | bytes 3145728 | tf_op jit(solution)/shard_map/local/pallas_call | solution.py:415
  47.4 1.0 %copy-done.1 = bf16[256,2048]{1,0:T(8,128)(2,1)} copy-done((bf16[256,2048]{1,0:T(8,128)(2,1)}, bf16[256,2048]{1,0:T(8,128)(2,1)S(1)}, u32[]{:S(2)}) %copy-start.1) | copy-done | bytes 1048600
  48.4 0.0 collective-permute-done.3.rest_3_
  48.4 0.0 collective-permute-done.4.rest_4_
  48.4 0.0 collective-permute-done.5.rest_5_
  48.5 0.0 collective-permute-done.6.rest_6_
  48.5 0.0 collective-permute-done.7.rest_7_
  48.5 2.3 %slots.1 = (f32[16,2048]{1,0:T(8,128)S(1)}, bf16[1,16,2048]{2,1,0:T(8,128)(2,1)S(1)}, bf16[1,16,2048]{2,1,0:T(8,128)(2,1)S(1)}, bf16[1,16,2048]{2,1,0:T(8,128)(2,1)S(1)}, bf16[1,16,2048]{2,1,0:T(8,128)(2,1)S(1)}) custom-call(s32[65]{0:T(128)S(1)} %copy-done.6, s32[32]{0:T(128)S(1)} %copy-done.7, s32[1]{0:T(128)} %bitcast.place, s32[1]{0:T(128)} %bitcast.4.line, ...), custom_call_target="tpu_custom_call" | custom-call | tf_op jit(solution)/shard_map/slots/pallas_call | solution.py:442
  50.8 0.0 copy-start.5
  50.8 0.6 %copy-done.5 = f32[16,2048]{1,0:T(8,128)} copy-done((f32[16,2048]{1,0:T(8,128)}, f32[16,2048]{1,0:T(8,128)S(1)}, u32[]{:S(2)}) %copy-start.5) | copy-done | bytes 131096
  51.4 1.6 %collective-permute-start.8 = (bf16[1,16,2048]{2,1,0:T(8,128)(2,1)S(1)}, bf16[1,16,2048]{2,1,0:T(8,128)(2,1)S(1)}, u32[]{:S(2)}, u32[]{:S(2)}) collective-permute-start(bf16[1,16,2048]{2,1,0:T(8,128)(2,1)S(1)} %get-tuple-element.45), channel_id=1, source_target_pairs={{0,1},{1,2},{2,3},{3,0},{4,5},{5,6},{6,7},{7,4},{8,9},{9,10},{10,1... | collective-permute-start | bytes 196616 | tf_op jit(solution)/shard_map/ppermute | solution.py:460
  53.0 2.6 %collective-permute-start.9 = (bf16[1,16,2048]{2,1,0:T(8,128)(2,1)S(1)}, bf16[1,16,2048]{2,1,0:T(8,128)(2,1)S(1)}, u32[]{:S(2)}, u32[]{:S(2)}) collective-permute-start(bf16[1,16,2048]{2,1,0:T(8,128)(2,1)S(1)} %get-tuple-element.46), channel_id=1, source_target_pairs={{0,2},{1,3},{2,0},{3,1},{4,6},{5,7},{6,4},{7,5},{8,10},{9,11},{10,... | collective-permute-start | bytes 196616 | tf_op jit(solution)/shard_map/ppermute | solution.py:460
  55.6 1.4 %collective-permute-start.10 = (bf16[1,16,2048]{2,1,0:T(8,128)(2,1)S(1)}, bf16[1,16,2048]{2,1,0:T(8,128)(2,1)S(1)}, u32[]{:S(2)}, u32[]{:S(2)}) collective-permute-start(bf16[1,16,2048]{2,1,0:T(8,128)(2,1)S(1)} %get-tuple-element.47), channel_id=1, source_target_pairs={{0,3},{1,0},{2,1},{3,2},{4,7},{5,4},{6,5},{7,6},{8,11},{9,8},{10,9... | collective-permute-start | bytes 196616 | tf_op jit(solution)/shard_map/ppermute | solution.py:460
  57.0 0.0 copy-done
  57.0 4.4 %output.1 = bf16[256,2048]{1,0:T(8,128)(2,1)} custom-call(bf16[256,2048]{1,0:T(8,128)(2,1)} %query.1, f32[256,2048]{1,0:T(8,128)} %copy-done, f32[16,2048]{1,0:T(8,128)} %copy-done.5, bf16[256,2048]{1,0:T(8,128)(2,1)} %copy-done.1), custom_call_target="tpu_custom_call" | custom-call | flops 805306368 | bytes 6291456 | tf_op jit(solution)/shard_map/output/pallas_call | solution.py:462
  61.4 0.0 collective-permute-done.8.refs_1_
  61.4 0.0 collective-permute-done.9.refs_2_
  61.4 0.0 collective-permute-done.10.refs_3_
  61.4 0.8 %widen.1 = f32[1,16,8192]{2,1,0:T(8,128)} custom-call(s32[1]{0:T(128)} %bitcast.4.line, bf16[1,16,2048]{2,1,0:T(8,128)(2,1)S(1)} %get-tuple-element.44.refs_0_, bf16[1,16,2048]{2,1,0:T(8,128)(2,1)S(1)} %collective-permute-done.8.refs_1_, bf16[1,16,2048]{2,1,0:T(8,128)(2,1)S(1)} %collective-permute-done.9.refs_2_, ...), custom_call_target="tpu_custom_call" | custom-call | tf_op jit(solution)/shard_map/widen/pallas_call | solution.py:475
  (13 shorter events, 0.0 us)
Async XLA Ops:
  1.7 5.8 %collective-permute-start = (bf16[128,2048]{1,0:T(8,128)(2,1)S(1)}, bf16[128,2048]{1,0:T(8,128)(2,1)S(1)}, u32[]{:S(2)}, u32[]{:S(2)}) collective-permute-start(bf16[128,2048]{1,0:T(8,128)(2,1)S(1)} %slice.3), channel_id=1, source_target_pairs={{0,4},{4,8},{8,12},{12,16},{16,20},{20,24},{24,28},{1,5},{5,9},{9,... | collective-permute-start | bytes 1572872 | tf_op jit(solution)/shard_map/ppermute | solution.py:352
  7.4 21.0 %copy-start.12 = (f32[16,128]{1,0:T(8,128)S(1)}, f32[16,128]{1,0:T(8,128)}, u32[]{:S(2)}) copy-start(f32[16,128]{1,0:T(8,128)} %resid.1) | copy-start | bytes 24580
  7.5 21.2 %copy-start.13 = (f32[16,128]{1,0:T(8,128)S(1)}, f32[16,128]{1,0:T(8,128)}, u32[]{:S(2)}) copy-start(f32[16,128]{1,0:T(8,128)} %rates.1) | copy-start | bytes 24580
  7.5 32.6 %copy-start.4 = (bf16[5,128,128]{2,1,0:T(8,128)(2,1)S(1)}, bf16[5,128,128]{2,1,0:T(8,128)(2,1)}, u32[]{:S(2)}) copy-start(bf16[5,128,128]{2,1,0:T(8,128)(2,1)} %get-tuple-element.28.masks) | copy-start | bytes 491524
  7.5 32.6 %copy-start.6 = (s32[65]{0:T(128)S(1)}, s32[65]{0:T(128)}, u32[]{:S(2)}) copy-start(s32[65]{0:T(128)} %offsets.5) | copy-start | bytes 784
  7.5 32.6 %copy-start.9 = (f32[2048]{0:T(1024)S(1)}, f32[2048]{0:T(1024)}, u32[]{:S(2)}) copy-start(f32[2048]{0:T(1024)} %param.15) | copy-start | bytes 24580
  7.5 32.6 %copy-start.10 = (f32[2,128,128]{2,1,0:T(8,128)S(1)}, f32[2,128,128]{2,1,0:T(8,128)}, u32[]{:S(2)}) copy-start(f32[2,128,128]{2,1,0:T(8,128)} %get-tuple-element.32.taps) | copy-start | bytes 393220
  7.5 0.8 %copy-start.11 = (bf16[128,2048]{1,0:T(8,128)(2,1)}, bf16[128,2048]{1,0:T(8,128)(2,1)S(1)}, u32[]{:S(2)}) copy-start(bf16[128,2048]{1,0:T(8,128)(2,1)S(1)} %collective-permute-done.halo) | copy-start | bytes 1572868
  20.7 11.8 %collective-permute-start.1 = (bf16[3,16,2048]{2,1,0:T(8,128)(2,1)}, bf16[3,16,2048]{2,1,0:T(8,128)(2,1)S(1)}, u32[]{:S(2)}, u32[]{:S(2)}) collective-permute-start(bf16[3,16,2048]{2,1,0:T(8,128)(2,1)} %get-tuple-element.35), channel_id=1, source_target_pairs={{0,4},{4,8},{8,12},{12,16},{16,20},{20,24},{24,28},{28,0},{1,5},{5... | collective-permute-start | bytes 589832 | tf_op jit(solution)/shard_map/ppermute | solution.py:413
  26.0 10.1 %collective-permute-start.2 = (bf16[3,16,2048]{2,1,0:T(8,128)(2,1)}, bf16[3,16,2048]{2,1,0:T(8,128)(2,1)S(1)}, u32[]{:S(2)}, u32[]{:S(2)}) collective-permute-start(bf16[3,16,2048]{2,1,0:T(8,128)(2,1)} %get-tuple-element.36), channel_id=1, source_target_pairs={{0,8},{4,12},{8,16},{12,20},{16,24},{20,28},{24,0},{28,4},{1,9},{5... | collective-permute-start | bytes 589832 | tf_op jit(solution)/shard_map/ppermute | solution.py:413
  28.8 19.6 %collective-permute-start.3 = (bf16[3,16,2048]{2,1,0:T(8,128)(2,1)}, bf16[3,16,2048]{2,1,0:T(8,128)(2,1)S(1)}, u32[]{:S(2)}, u32[]{:S(2)}) collective-permute-start(bf16[3,16,2048]{2,1,0:T(8,128)(2,1)} %get-tuple-element.37), channel_id=1, source_target_pairs={{0,12},{4,16},{8,20},{12,24},{16,28},{20,0},{24,4},{28,8},{1,13},{... | collective-permute-start | bytes 589832 | tf_op jit(solution)/shard_map/ppermute | solution.py:413
  31.2 17.2 %collective-permute-start.4 = (bf16[3,16,2048]{2,1,0:T(8,128)(2,1)}, bf16[3,16,2048]{2,1,0:T(8,128)(2,1)S(1)}, u32[]{:S(2)}, u32[]{:S(2)}) collective-permute-start(bf16[3,16,2048]{2,1,0:T(8,128)(2,1)} %get-tuple-element.38), channel_id=1, source_target_pairs={{0,16},{4,20},{8,24},{12,28},{16,0},{20,4},{24,8},{28,12},{1,17},{... | collective-permute-start | bytes 589832 | tf_op jit(solution)/shard_map/ppermute | solution.py:413
  31.8 16.7 %collective-permute-start.5 = (bf16[3,16,2048]{2,1,0:T(8,128)(2,1)}, bf16[3,16,2048]{2,1,0:T(8,128)(2,1)S(1)}, u32[]{:S(2)}, u32[]{:S(2)}) collective-permute-start(bf16[3,16,2048]{2,1,0:T(8,128)(2,1)} %get-tuple-element.39), channel_id=1, source_target_pairs={{0,20},{4,24},{8,28},{12,0},{16,4},{20,8},{24,12},{28,16},{1,21},{... | collective-permute-start | bytes 589832 | tf_op jit(solution)/shard_map/ppermute | solution.py:413
  32.5 16.0 %collective-permute-start.6 = (bf16[3,16,2048]{2,1,0:T(8,128)(2,1)}, bf16[3,16,2048]{2,1,0:T(8,128)(2,1)S(1)}, u32[]{:S(2)}, u32[]{:S(2)}) collective-permute-start(bf16[3,16,2048]{2,1,0:T(8,128)(2,1)} %get-tuple-element.40), channel_id=1, source_target_pairs={{0,24},{4,28},{8,0},{12,4},{16,8},{20,12},{24,16},{28,20},{1,25},{... | collective-permute-start | bytes 589832 | tf_op jit(solution)/shard_map/ppermute | solution.py:413
  36.2 12.3 %collective-permute-start.7 = (bf16[3,16,2048]{2,1,0:T(8,128)(2,1)}, bf16[3,16,2048]{2,1,0:T(8,128)(2,1)S(1)}, u32[]{:S(2)}, u32[]{:S(2)}) collective-permute-start(bf16[3,16,2048]{2,1,0:T(8,128)(2,1)} %get-tuple-element.41), channel_id=1, source_target_pairs={{0,28},{4,0},{8,4},{12,8},{16,12},{20,16},{24,20},{28,24},{1,29},{... | collective-permute-start | bytes 589832 | tf_op jit(solution)/shard_map/ppermute | solution.py:413
  40.1 1.2 %copy-start.8 = (bf16[256,2048]{1,0:T(8,128)(2,1)S(1)}, bf16[256,2048]{1,0:T(8,128)(2,1)}, u32[]{:S(2)}) copy-start(bf16[256,2048]{1,0:T(8,128)(2,1)} %get-tuple-element.31.mixed) | copy-start | bytes 3145732
  41.3 7.1 %copy-start.2 = (f32[16,2048]{1,0:T(8,128)S(1)}, f32[16,2048]{1,0:T(8,128)}, u32[]{:S(2)}) copy-start(f32[16,2048]{1,0:T(8,128)} %get-tuple-element.29.rates.rest_8_) | copy-start | bytes 393220
  41.3 7.2 %copy-start.3 = (bf16[3,16,2048]{2,1,0:T(8,128)(2,1)S(1)}, bf16[3,16,2048]{2,1,0:T(8,128)(2,1)}, u32[]{:S(2)}) copy-start(bf16[3,16,2048]{2,1,0:T(8,128)(2,1)} %get-tuple-element.34.rest_0_) | copy-start | bytes 589828
  41.3 7.2 %copy-start.7 = (s32[32]{0:T(128)S(1)}, s32[32]{0:T(128)}, u32[]{:S(2)}) copy-start(s32[32]{0:T(128)} %owners.3) | copy-start | bytes 388
  47.4 1.0 %copy-start.1 = (bf16[256,2048]{1,0:T(8,128)(2,1)}, bf16[256,2048]{1,0:T(8,128)(2,1)S(1)}, u32[]{:S(2)}) copy-start(bf16[256,2048]{1,0:T(8,128)(2,1)S(1)} %get-tuple-element.43.weight) | copy-start | bytes 3145732
  48.4 8.6 %copy-start = (f32[256,2048]{1,0:T(8,128)}, f32[256,2048]{1,0:T(8,128)S(1)}, u32[]{:S(2)}) copy-start(f32[256,2048]{1,0:T(8,128)S(1)} %get-tuple-element.33.rest_9_.local) | copy-start | bytes 6291460
  50.8 0.7 %copy-start.5 = (f32[16,2048]{1,0:T(8,128)}, f32[16,2048]{1,0:T(8,128)S(1)}, u32[]{:S(2)}) copy-start(f32[16,2048]{1,0:T(8,128)S(1)} %get-tuple-element.42.entering) | copy-start | bytes 393220
  51.4 10.0 %collective-permute-start.8 = (bf16[1,16,2048]{2,1,0:T(8,128)(2,1)S(1)}, bf16[1,16,2048]{2,1,0:T(8,128)(2,1)S(1)}, u32[]{:S(2)}, u32[]{:S(2)}) collective-permute-start(bf16[1,16,2048]{2,1,0:T(8,128)(2,1)S(1)} %get-tuple-element.45), channel_id=1, source_target_pairs={{0,1},{1,2},{2,3},{3,0},{4,5},{5,6},{6,7},{7,4},{8,9},{9,10},{10,1... | collective-permute-start | bytes 196616 | tf_op jit(solution)/shard_map/ppermute | solution.py:460
  53.0 8.4 %collective-permute-start.9 = (bf16[1,16,2048]{2,1,0:T(8,128)(2,1)S(1)}, bf16[1,16,2048]{2,1,0:T(8,128)(2,1)S(1)}, u32[]{:S(2)}, u32[]{:S(2)}) collective-permute-start(bf16[1,16,2048]{2,1,0:T(8,128)(2,1)S(1)} %get-tuple-element.46), channel_id=1, source_target_pairs={{0,2},{1,3},{2,0},{3,1},{4,6},{5,7},{6,4},{7,5},{8,10},{9,11},{10,... | collective-permute-start | bytes 196616 | tf_op jit(solution)/shard_map/ppermute | solution.py:460
  55.6 5.8 %collective-permute-start.10 = (bf16[1,16,2048]{2,1,0:T(8,128)(2,1)S(1)}, bf16[1,16,2048]{2,1,0:T(8,128)(2,1)S(1)}, u32[]{:S(2)}, u32[]{:S(2)}) collective-permute-start(bf16[1,16,2048]{2,1,0:T(8,128)(2,1)S(1)} %get-tuple-element.47), channel_id=1, source_target_pairs={{0,3},{1,0},{2,1},{3,2},{4,7},{5,4},{6,5},{7,6},{8,11},{9,8},{10,9... | collective-permute-start | bytes 196616 | tf_op jit(solution)/shard_map/ppermute | solution.py:460
where the time goes:
time: 62.7 us; the launch traced here: 62.3 us
  Pallas kernels  29.3 us (47%)
  starting transfers between devices  27 us (43%)
  local copies, waits for them, and re-layouts  5.15 us (8%)
  between operations  0.86 us (1%)
    ppermute x7, starting transfers between devices, per_device(): got.append(lax.ppermute(ends[d], 'ctx', route))  19 us
    pallas_call x1, Pallas kernels, per_device(): pl.pallas_call(functools.partial(states_kernel, cap, size), grid=(width /...  12.4 us
    pallas_call x1, Pallas kernels, per_device(): pl.pallas_call(functools.partial(local_kernel, size), grid=(width // bloc...  6.1 us
    ppermute x3, starting transfers between devices, per_device(): arrived.append(lax.ppermute(picked[d], 'ch', route))  5.58 us
    pallas_call x1, Pallas kernels, per_device(): pl.pallas_call(functools.partial(output_kernel, size), grid=(width // blo...  4.37 us
    unnamed x28, local copies, waits for them, and re-layouts  3.69 us
    pallas_call x1, Pallas kernels, per_device(): pl.pallas_call(functools.partial(prepare_kernel, cap, peers, size), in_sp...  3.32 us
    ppermute x1, starting transfers between devices, per_device(): lax.ppermute(value[length - TAPS:], 'ctx', [(i, i + 1) for i in range(pee...  2.39 us
  transfers between devices with their start and end apart: 11, of which 0 were waited for; matrix products, arithmetic and copies ran while one was open for 1% of the time, Pallas kernels for 22%

commit v1 on v0

--- a/solution.py
+++ b/solution.py
@@ -117,7 +117,8 @@
 
     def mark(k, carry):
         doc = d0 + k
-        order = lax.rem(doc - owners[0] + docs, docs)
+        order = doc - owners[0]
+        order = jnp.where(order < 0, order + docs, order)
         start = offsets[jnp.minimum(doc, docs)] - begin
         end = offsets[jnp.minimum(doc + 1, docs)] - 1 - begin
 
@@ -171,6 +172,17 @@
         gains_out[:, at] = gain(wide)
 
 
+def second_kernel(size, value, key, rows, masks, mixed_out, circulants):
+    per_tile = LANES // size
+    for tile in range(value.shape[1] // LANES):
+        at = slice(tile * LANES, (tile + 1) * LANES)
+        blocks = []
+        for g in range(tile * per_tile, (tile + 1) * per_tile):
+            blocks.append(circulant(rows[g : g + 1]))
+            circulants[g] = blocks[-1]
+        mixed_out[:, at] = filtered(blocks, masks, 2, 3, value[:, at], key[:, at])
+
+
 def states_kernel(
     cap,
     size,
@@ -180,8 +192,9 @@
     halo,
     value,
     key,
-    rows,
+    circulants,
     masks,
+    second,
     rates,
     gains,
     mixed_out,
@@ -189,7 +202,7 @@
 ):
     ends_out, (wide, history) = rest[:-2], rest[-2:]
     poles, width = rates.shape
-    length, block = value.shape
+    length, block = 2 * TAPS, value.shape[1]
     peers = len(ends_out)
     step = pl.program_id(0)
     per_tile = LANES // size
@@ -197,17 +210,12 @@
     for tile in range(block // LANES):
         at = slice(tile * LANES, (tile + 1) * LANES)
         spot = pl.ds(pl.multiple_of(step * block + tile * LANES, LANES), LANES)
-        x = value[:, at]
-        window = jnp.concatenate([halo[:, at], x[:TAPS]], axis=0)
-        blocks = [
-            circulant(rows[tile * per_tile + g : tile * per_tile + g + 1]) for g in range(per_tile)
-        ]
-        mixed0 = filtered(blocks, masks, 0, 1, window, key[:TAPS, at])
-        mixed1 = filtered(blocks, masks, 2, 3, x, key[TAPS:, at])
-        mixed_out[:TAPS, at] = mixed0
-        mixed_out[TAPS:, at] = mixed1
-        wide[:TAPS, spot] = mixed0.astype(F32)
-        wide[TAPS:, spot] = mixed1.astype(F32)
+        window = jnp.concatenate([halo[:, at], value[:, at]], axis=0)
+        blocks = [circulants[tile * per_tile + g] for g in range(per_tile)]
+        mixed = filtered(blocks, masks, 0, 1, window, key[:, at])
+        mixed_out[:, at] = mixed
+        wide[:TAPS, spot] = mixed.astype(F32)
+        wide[TAPS:, spot] = second[:, at].astype(F32)
 
     @pl.when(step == pl.num_programs(0) - 1)
     def run():
@@ -234,9 +242,9 @@
 
 
 def local_kernel(
-    size, offsets, place, mixed, masks, taps, skip, rates, resid, local_out, weight_out, limit
+    size, offsets, place, first, second, masks, taps, skip, rates, resid, local_out, weight_out, limit
 ):
-    length, block = mixed.shape
+    length, block = 2 * TAPS, first.shape[1]
     begin = place[0] * length
     step = pl.program_id(0)
     per_tile = LANES // size
@@ -250,7 +258,7 @@
     lane_group = iota((TAPS, LANES), 1) // size
     for tile in range(block // LANES):
         at = slice(tile * LANES, (tile + 1) * LANES)
-        x = mixed[:, at]
+        x = jnp.concatenate([first[:, at], second[:, at]], axis=0)
         acc0 = jnp.zeros((TAPS, LANES), F32)
         acc1 = jnp.zeros((TAPS, LANES), F32)
         for g in range(per_tile):
@@ -260,7 +268,8 @@
             y1 = dot(jnp.concatenate([a * masks[2] + b * masks[4], a * masks[3]], axis=1), x)
             acc0 = jnp.where(lane_group == g, y0, acc0)
             acc1 = jnp.where(lane_group == g, y1, acc1)
-        local_out[:, at] = jnp.concatenate([acc0, acc1], axis=0) + skip[:, at] * x.astype(F32)
+        total = jnp.concatenate([acc0, acc1], axis=0) + skip[:, at] * x.astype(F32)
+        local_out[:, at] = total.astype(BF16)
         weight = jnp.exp(-rates[:, at] * (t + 1).astype(F32)) * resid[:, at]
         weight = jnp.where(t < limit[0], weight, 0.0)
         weight_out[:, at] = weight.astype(BF16)
@@ -326,7 +335,7 @@
         at = slice(first, first + tile)
         spread_out = jnp.concatenate([entering[:, at].astype(BF16)] * (tile // size), axis=0) * kept
         fix = dot(weight[:, at], spread_out)
-        out[:, at] = (query[:, at].astype(F32) * (local[:, at] + fix)).astype(BF16)
+        out[:, at] = (query[:, at].astype(F32) * (local[:, at].astype(F32) + fix)).astype(BF16)
 
 
 def widen_kernel(line, *refs):
@@ -358,8 +367,8 @@
 
     block = min(width, BLOCK)
 
-    def lanes(height):
-        return pl.BlockSpec((height, block), lambda i: (0, i))
+    def lanes(height, size=block):
+        return pl.BlockSpec((height, size), lambda i: (0, i))
 
     vmem = pl.BlockSpec(memory_space=pltpu.VMEM)
     hbm = pl.BlockSpec(memory_space=pl.ANY)
@@ -381,53 +390,80 @@
         name="prepare",
     )(offsets, owners, place, filt, rates, resid)
 
-    mixed, *ends = pl.pallas_call(
+    def half(row, size=block):
+        return pl.BlockSpec((TAPS, size), lambda i: (row, i))
+
+    second, circulants = pl.pallas_call(
+        functools.partial(second_kernel, size),
+        grid=(width // block,),
+        in_specs=[
+            lanes(length),
+            half(1),
+            pl.BlockSpec((block // size, TAPS), lambda i: (i, 0)),
+            whole((5, TAPS, TAPS)),
+        ],
+        out_specs=[half(0), pl.BlockSpec((block // size, TAPS, TAPS), lambda i: (i, 0, 0))],
+        out_shape=[
+            jax.ShapeDtypeStruct((TAPS, width), BF16),
+            jax.ShapeDtypeStruct((groups, TAPS, TAPS), BF16),
+        ],
+        compiler_params=params(1, 60),
+        cost_estimate=pl.CostEstimate(
+            flops=16 * length * length * width, bytes_accessed=7 * length * width, transcendentals=0
+        ),
+        name="second",
+    )(value, key, rows, masks)
+
+    first, *ends = pl.pallas_call(
         functools.partial(states_kernel, cap, size),
         grid=(width // block,),
         in_specs=[
             SMEM,
             SMEM,
             SMEM,
-            lanes(TAPS),
-            lanes(length),
-            lanes(length),
-            pl.BlockSpec((block // size, TAPS), lambda i: (i, 0)),
+            half(0),
+            half(0),
+            half(0),
+            pl.BlockSpec((block // size, TAPS, TAPS), lambda i: (i, 0, 0)),
             whole((5, TAPS, TAPS)),
+            half(0),
             whole((poles, width)),
             whole((poles, width)),
         ],
-        out_specs=[lanes(length)] + [whole((cap + 1, poles, width))] * peers,
-        out_shape=[jax.ShapeDtypeStruct((length, width), BF16)]
+        out_specs=[half(0)] + [whole((cap + 1, poles, width))] * peers,
+        out_shape=[jax.ShapeDtypeStruct((TAPS, width), BF16)]
         + [jax.ShapeDtypeStruct((cap + 1, poles, width), BF16)] * peers,
         scratch_shapes=[
             pltpu.VMEM((length, width), F32),
             pltpu.VMEM((length, poles, block), F32),
         ],
-        compiler_params=params(1, 56),
+        compiler_params=params(1, 50),
         name="states",
-    )(place, keep, last, halo, value, key, rows, masks, rates_wide, gains_wide)
+    )(place, keep, last, halo, value, key, circulants, masks, second, rates_wide, gains_wide)
 
     got = [ends[0]]
     for d in range(1, peers):
         route = [(i, (i + d) % peers) for i in range(peers)]
         got.append(lax.ppermute(ends[d], "ctx", route))
 
+    broad = min(width, 8 * LANES)
     local, weight = pl.pallas_call(
         functools.partial(local_kernel, size),
-        grid=(width // block,),
+        grid=(width // broad,),
         in_specs=[
             SMEM,
             SMEM,
-            lanes(length),
+            half(0, broad),
+            half(0, broad),
             whole((5, TAPS, TAPS)),
-            pl.BlockSpec((2, block // size, TAPS), lambda i: (0, i, 0)),
-            lanes(1),
-            lanes(1),
-            lanes(1),
-        ],
-        out_specs=[lanes(length)] * 2,
+            pl.BlockSpec((2, broad // size, TAPS), lambda i: (0, i, 0)),
+            lanes(1, broad),
+            lanes(1, broad),
+            lanes(1, broad),
+        ],
+        out_specs=[lanes(length, broad)] * 2,
         out_shape=[
-            jax.ShapeDtypeStruct((length, width), F32),
+            jax.ShapeDtypeStruct((length, width), BF16),
             jax.ShapeDtypeStruct((length, width), BF16),
         ],
         scratch_shapes=[pltpu.SMEM((1,), jnp.int32)],
@@ -436,7 +472,7 @@
             flops=32 * length * length * width, bytes_accessed=6 * length * width, transcendentals=0
         ),
         name="local",
-    )(offsets, place, mixed, masks, taps, skip.reshape(1, width), rates_flat, resid_flat)
+    )(offsets, place, first, second, masks, taps, skip.reshape(1, width), rates_flat, resid_flat)
 
     per_line = slots // lines
     entering, *picked = pl.pallas_call(
@@ -459,11 +495,12 @@
         route = [(i, (i + d) % lines) for i in range(lines)]
         arrived.append(lax.ppermute(picked[d], "ch", route))
 
+    thin = min(width, 8 * LANES)
     output = pl.pallas_call(
         functools.partial(output_kernel, size),
-        grid=(width // block,),
-        in_specs=[lanes(length), lanes(length), lanes(poles), lanes(length)],
-        out_specs=lanes(length),
+        grid=(width // thin,),
+        in_specs=[lanes(length, thin), lanes(length, thin), lanes(poles, thin), lanes(length, thin)],
+        out_specs=lanes(length, thin),
         out_shape=jax.ShapeDtypeStruct((length, width), BF16),
         compiler_params=params(1, 60),
         cost_estimate=pl.CostEstimate(

time: 62.7 us -> 61.4 us (0.979)
  starting transfers between devices: 27 us -> 19.8 us
  waiting for transfers between devices: 0.03 us -> 4.81 us
  Pallas kernels: 29.3 us -> 30.1 us
    ppermute x7, starting transfers between devices: 19 us -> 12.7 us  [per_device(): got.append(lax.ppermute(ends[d], 'ctx', route))]
    ppermute x3, waiting for transfers between devices: 0.01 us -> 3.96 us  [per_device(): arrived.append(lax.ppermute(picked[d], 'ch', route))]
    pallas_call x2 -> x3, Pallas kernels: 10.5 us -> 14.2 us  [the longest x1 5.76 us: per_device(): pl.pallas_call(functools.partial(second_kernel, size), grid=(width // blo...]
    pallas_call x1, Pallas kernels: 12.4 us -> 9.47 us  [per_device(): pl.pallas_call(functools.partial(states_kernel, cap, size), grid=(width /...]
    ppermute x3, starting transfers between devices: 5.58 us -> 4.64 us  [per_device(): arrived.append(lax.ppermute(picked[d], 'ch', route))]
    ppermute x7, waiting for transfers between devices: 0.02 us -> 0.85 us  [per_device(): got.append(lax.ppermute(ends[d], 'ctx', route))]
    unnamed x28 -> x32, local copies, waits for them, and re-layouts: 3.69 us -> 3.6 us
  transfers between devices with their start and end apart: 11 -> 11, of which waited for: 0 -> 3; matrix products, arithmetic and copies ran while one was open for 1% -> 1% of each run, Pallas kernels for 22% -> 29%
where the time goes in v1:
time: 61.4 us; the launch traced here: 60.7 us
  Pallas kernels  30.1 us (49%)
  starting transfers between devices  19.8 us (32%)
  local copies, waits for them, and re-layouts  5.06 us (8%)
  waiting for transfers between devices  4.81 us (8%)
  between operations  0.89 us (1%)
    ppermute x7, starting transfers between devices, per_device(): got.append(lax.ppermute(ends[d], 'ctx', route))  12.7 us
    pallas_call x1, Pallas kernels, per_device(): pl.pallas_call(functools.partial(states_kernel, cap, size), grid=(width /...  9.47 us
    pallas_call x1, Pallas kernels, per_device(): pl.pallas_call(functools.partial(second_kernel, size), grid=(width // blo...  5.76 us
    pallas_call x1, Pallas kernels, per_device(): pl.pallas_call(functools.partial(local_kernel, size), grid=(width // broa...  5.46 us
    ppermute x3, starting transfers between devices, per_device(): arrived.append(lax.ppermute(picked[d], 'ch', route))  4.64 us
    ppermute x3, waiting for transfers between devices, per_device(): arrived.append(lax.ppermute(picked[d], 'ch', route))  3.96 us
    unnamed x32, local copies, waits for them, and re-layouts  3.6 us
    pallas_call x1, Pallas kernels, per_device(): pl.pallas_call(functools.partial(prepare_kernel, cap, peers, size), in_sp...  3.31 us
  transfers between devices with their start and end apart: 11, of which 3 were waited for; matrix products, arithmetic and copies ran while one was open for 1% of the time, Pallas kernels for 29%

profile of v1, /device:TPU:0, one launch (start us, length us, event | category | flops | bytes accessed | tf_op | source)
XLA Modules:
  0.0 60.7 jit_solution(7913609484320065976)
XLA Ops:
  0.6 1.1 %slice.3 = bf16[128,2048]{1,0:T(8,128)(2,1)S(1)} slice(bf16[256,2048]{1,0:T(8,128)(2,1)} %value.3), slice={[128:256], [0:2048]} | slice | bytes 1048576 | tf_op jit(solution)/shard_map/slice | solution.py:362
  1.7 2.4 %collective-permute-start = (bf16[128,2048]{1,0:T(8,128)(2,1)S(1)}, bf16[128,2048]{1,0:T(8,128)(2,1)S(1)}, u32[]{:S(2)}, u32[]{:S(2)}) collective-permute-start(bf16[128,2048]{1,0:T(8,128)(2,1)S(1)} %slice.3), channel_id=1, source_target_pairs={{0,4},{4,8},{8,12},{12,16},{16,20},{20,24},{24,28},{1,5},{5,9},{9,... | collective-permute-start | bytes 1572872 | tf_op jit(solution)/shard_map/ppermute | solution.py:361
  4.1 3.3 %prepare.1 = (f32[16,2048]{1,0:T(8,128)}, f32[16,2048]{1,0:T(8,128)}, f32[128,128]{1,0:T(8,128)}, bf16[5,128,128]{2,1,0:T(8,128)(2,1)}, f32[2,128,128]{2,1,0:T(8,128)}, /*index=5*/f32[256]{0:T(256)}, s32[16]{0:T(128)}) custom-call(s32[65]{0:T(128)} %offsets.5, s32[32]{0:T(128)} %owners.3, s32[1]{0:T(128)} %bitcast.place, bf16[128,128]{1,0:T(8,128)(2,1)} %filt.1, ...), custom_call_target="tpu_custom_call" | custom-call | flops 1073741824 | bytes 1048576 | tf_op jit(solution)/shard_map/prepare/pallas_call | solution.py:375
  7.5 0.0 copy-start.5
  7.5 0.0 copy-start.6
  7.5 0.0 copy-start.8
  7.5 0.0 copy-start.11
  7.5 0.0 copy-start.14
  7.5 0.0 copy-start.15
  7.5 5.8 %second.1 = (bf16[128,2048]{1,0:T(8,128)(2,1)}, bf16[128,128,128]{2,1,0:T(8,128)(2,1)}) custom-call(bf16[256,2048]{1,0:T(8,128)(2,1)} %value.3, bf16[256,2048]{1,0:T(8,128)(2,1)} %key.3, f32[128,128]{1,0:T(8,128)} %get-tuple-element.29.rows, bf16[5,128,128]{2,1,0:T(8,128)(2,1)} %get-tuple-element.30.masks), custom_call_target="tpu_custom_call" | custom-call | flops 2147483648 | bytes 3670016 | tf_op jit(solution)/shard_map/second/pallas_call | solution.py:396
  13.3 0.0 collective-permute-done.halo
  13.3 0.0 copy-done.2
  13.3 0.0 copy-done.5
  13.4 0.0 copy-start.3
  13.4 1.0 %copy-done.3 = bf16[128,2048]{1,0:T(8,128)(2,1)S(1)} copy-done((bf16[128,2048]{1,0:T(8,128)(2,1)S(1)}, bf16[128,2048]{1,0:T(8,128)(2,1)}, u32[]{:S(2)}) %copy-start.3) | copy-done | bytes 524312
  14.4 9.5 %states.1 = (bf16[128,2048]{1,0:T(8,128)(2,1)S(1)}, bf16[3,16,2048]{2,1,0:T(8,128)(2,1)S(1)}, bf16[3,16,2048]{2,1,0:T(8,128)(2,1)S(1)}, bf16[3,16,2048]{2,1,0:T(...) custom-call(s32[1]{0:T(128)} %bitcast.place, ...), custom_call_target="tpu_custom_call" | custom-call | tf_op jit(solution)/shard_map/states/pallas_call | solution.py:417
  23.9 2.6 %collective-permute-start.1 = (bf16[3,16,2048]{2,1,0:T(8,128)(2,1)S(1)}, bf16[3,16,2048]{2,1,0:T(8,128)(2,1)S(1)}, u32[]{:S(2)}, u32[]{:S(2)}) collective-permute-start(bf16[3,16,2048]{2,1,0:T(8,128)(2,1)S(1)} %get-tuple-element.39), channel_id=1, source_target_pairs={{0,4},{4,8},{8,12},{12,16},{16,20},{20,24},{24,28},{28,0},{1,5},{5... | collective-permute-start | bytes 589832 | tf_op jit(solution)/shard_map/ppermute | solution.py:447
  26.5 1.5 %collective-permute-start.2 = (bf16[3,16,2048]{2,1,0:T(8,128)(2,1)S(1)}, bf16[3,16,2048]{2,1,0:T(8,128)(2,1)S(1)}, u32[]{:S(2)}, u32[]{:S(2)}) collective-permute-start(bf16[3,16,2048]{2,1,0:T(8,128)(2,1)S(1)} %get-tuple-element.40), channel_id=1, source_target_pairs={{0,8},{4,12},{8,16},{12,20},{16,24},{20,28},{24,0},{28,4},{1,9},{5... | collective-permute-start | bytes 589832 | tf_op jit(solution)/shard_map/ppermute | solution.py:447
  28.0 0.1 copy.13
  28.1 0.1 reshape.21.rates
  28.2 0.1 copy.14
  28.3 0.1 reshape.22.resid
  28.4 0.9 %collective-permute-start.3 = (bf16[3,16,2048]{2,1,0:T(8,128)(2,1)S(1)}, bf16[3,16,2048]{2,1,0:T(8,128)(2,1)S(1)}, u32[]{:S(2)}, u32[]{:S(2)}) collective-permute-start(bf16[3,16,2048]{2,1,0:T(8,128)(2,1)S(1)} %get-tuple-element.41), channel_id=1, source_target_pairs={{0,12},{4,16},{8,20},{12,24},{16,28},{20,0},{24,4},{28,8},{1,13},{... | collective-permute-start | bytes 589832 | tf_op jit(solution)/shard_map/ppermute | solution.py:447
  29.3 0.5 collective-permute-start.4
  29.8 0.4 collective-permute-start.5
  30.2 0.0 collective-permute-done.1.rest_1_
  30.2 3.7 %collective-permute-start.6 = (bf16[3,16,2048]{2,1,0:T(8,128)(2,1)S(1)}, bf16[3,16,2048]{2,1,0:T(8,128)(2,1)S(1)}, u32[]{:S(2)}, u32[]{:S(2)}) collective-permute-start(bf16[3,16,2048]{2,1,0:T(8,128)(2,1)S(1)} %get-tuple-element.44), channel_id=1, source_target_pairs={{0,24},{4,28},{8,0},{12,4},{16,8},{20,12},{24,16},{28,20},{1,25},{... | collective-permute-start | bytes 589832 | tf_op jit(solution)/shard_map/ppermute | solution.py:447
  33.9 0.8 %collective-permute-done.2.rest_2_ = bf16[3,16,2048]{2,1,0:T(8,128)(2,1)S(1)} collective-permute-done((bf16[3,16,2048]{2,1,0:T(8,128)(2,1)S(1)}, bf16[3,16,2048]{2,1,0:T(8,128)(2,1)S(1)}, u32[]{:S(2)}, u32[]{:S(2)}) %collective-permute-start.2) | collective-permute-done | bytes 196640 | tf_op jit(solution)/shard_map/ppermute | solution.py:447
  34.8 3.1 %collective-permute-start.7 = (bf16[3,16,2048]{2,1,0:T(8,128)(2,1)S(1)}, bf16[3,16,2048]{2,1,0:T(8,128)(2,1)S(1)}, u32[]{:S(2)}, u32[]{:S(2)}) collective-permute-start(bf16[3,16,2048]{2,1,0:T(8,128)(2,1)S(1)} %get-tuple-element.45), channel_id=1, source_target_pairs={{0,28},{4,0},{8,4},{12,8},{16,12},{20,16},{24,20},{28,24},{1,29},{... | collective-permute-start | bytes 589832 | tf_op jit(solution)/shard_map/ppermute | solution.py:447
  37.9 0.9 %copy-done.13 = f32[2,128,128]{2,1,0:T(8,128)S(1)} copy-done((f32[2,128,128]{2,1,0:T(8,128)S(1)}, f32[2,128,128]{2,1,0:T(8,128)}, u32[]{:S(2)}) %copy-start.13) | copy-done | bytes 131096
  38.8 5.5 %local.1 = (bf16[256,2048]{1,0:T(8,128)(2,1)S(1)}, bf16[256,2048]{1,0:T(8,128)(2,1)S(1)}) custom-call(s32[65]{0:T(128)S(1)} %copy-done.9, s32[1]{0:T(128)} %bitcast.place, bf16[128,2048]{1,0:T(8,128)(2,1)S(1)} %get-tuple-element.35.first, bf16[128,2048]{1,0:T(8,128)(2,1)S(1)} %copy-done.4, bf16[5,128,128]{2,1,0:T(8,128)(2,1)S(1)} %copy-done.5, ...), custom_call_target="tpu_custom_call" | custom-call | flops 4294967296 | bytes 3145728 | tf_op jit(solution)/shard_map/local/pallas_call | solution.py:450
  44.3 1.0 %copy-done.1 = bf16[256,2048]{1,0:T(8,128)(2,1)} copy-done((bf16[256,2048]{1,0:T(8,128)(2,1)}, bf16[256,2048]{1,0:T(8,128)(2,1)S(1)}, u32[]{:S(2)}) %copy-start.1) | copy-done | bytes 1048600
  45.2 0.0 collective-permute-done.3.rest_3_
  45.2 0.0 collective-permute-done.4.rest_4_
  45.2 0.0 collective-permute-done.5.rest_5_
  45.2 0.0 collective-permute-done.6.rest_6_
  45.2 0.0 collective-permute-done.7.rest_7_
  45.3 2.3 %slots.1 = (f32[16,2048]{1,0:T(8,128)S(1)}, bf16[1,16,2048]{2,1,0:T(8,128)(2,1)S(1)}, bf16[1,16,2048]{2,1,0:T(8,128)(2,1)S(1)}, bf16[1,16,2048]{2,1,0:T(8,128)(2,1)S(1)}, bf16[1,16,2048]{2,1,0:T(8,128)(2,1)S(1)}) custom-call(s32[65]{0:T(128)S(1)} %copy-done.9, s32[32]{0:T(128)S(1)} %copy-done.10, s32[1]{0:T(128)} %bitcast.place, s32[1]{0:T(128)} %bitcast.4.line, ...), custom_call_target="tpu_custom_call" | custom-call | tf_op jit(solution)/shard_map/slots/pallas_call | solution.py:478
  47.5 0.0 copy-start.7
  47.6 0.6 %copy-done.7 = f32[16,2048]{1,0:T(8,128)} copy-done((f32[16,2048]{1,0:T(8,128)}, f32[16,2048]{1,0:T(8,128)S(1)}, u32[]{:S(2)}) %copy-start.7) | copy-done | bytes 131096
  48.2 3.6 %collective-permute-start.10 = (bf16[1,16,2048]{2,1,0:T(8,128)(2,1)S(1)}, bf16[1,16,2048]{2,1,0:T(8,128)(2,1)S(1)}, u32[]{:S(2)}, u32[]{:S(2)}) collective-permute-start(bf16[1,16,2048]{2,1,0:T(8,128)(2,1)S(1)} %get-tuple-element.51), channel_id=1, source_target_pairs={{0,3},{1,0},{2,1},{3,2},{4,7},{5,4},{6,5},{7,6},{8,11},{9,8},{10,9... | collective-permute-start | bytes 196616 | tf_op jit(solution)/shard_map/ppermute | solution.py:496
  51.8 0.0 collective-permute-start.8
  51.8 1.1 %collective-permute-start.9 = (bf16[1,16,2048]{2,1,0:T(8,128)(2,1)S(1)}, bf16[1,16,2048]{2,1,0:T(8,128)(2,1)S(1)}, u32[]{:S(2)}, u32[]{:S(2)}) collective-permute-start(bf16[1,16,2048]{2,1,0:T(8,128)(2,1)S(1)} %get-tuple-element.50), channel_id=1, source_target_pairs={{0,2},{1,3},{2,0},{3,1},{4,6},{5,7},{6,4},{7,5},{8,10},{9,11},{10,... | collective-permute-start | bytes 196616 | tf_op jit(solution)/shard_map/ppermute | solution.py:496
  52.8 3.0 %output.1 = bf16[256,2048]{1,0:T(8,128)(2,1)} custom-call(bf16[256,2048]{1,0:T(8,128)(2,1)} %query.1, bf16[256,2048]{1,0:T(8,128)(2,1)} %copy-done, f32[16,2048]{1,0:T(8,128)} %copy-done.7, bf16[256,2048]{1,0:T(8,128)(2,1)} %copy-done.1), custom_call_target="tpu_custom_call" | custom-call | flops 805306368 | bytes 6291456 | tf_op jit(solution)/shard_map/output/pallas_call | solution.py:499
  55.9 0.0 collective-permute-done.10.refs_3_
  55.9 2.7 %collective-permute-done.8.refs_1_ = bf16[1,16,2048]{2,1,0:T(8,128)(2,1)S(1)} collective-permute-done((bf16[1,16,2048]{2,1,0:T(8,128)(2,1)S(1)}, bf16[1,16,2048]{2,1,0:T(8,128)(2,1)S(1)}, u32[]{:S(2)}, u32[]{:S(2)}) %collective-permute-start.8) | collective-permute-done | bytes 65568 | tf_op jit(solution)/shard_map/ppermute | solution.py:496
  58.6 1.2 %collective-permute-done.9.refs_2_ = bf16[1,16,2048]{2,1,0:T(8,128)(2,1)S(1)} collective-permute-done((bf16[1,16,2048]{2,1,0:T(8,128)(2,1)S(1)}, bf16[1,16,2048]{2,1,0:T(8,128)(2,1)S(1)}, u32[]{:S(2)}, u32[]{:S(2)}) %collective-permute-start.9) | collective-permute-done | bytes 65568 | tf_op jit(solution)/shard_map/ppermute | solution.py:496
  59.8 0.8 %widen.1 = f32[1,16,8192]{2,1,0:T(8,128)} custom-call(s32[1]{0:T(128)} %bitcast.4.line, bf16[1,16,2048]{2,1,0:T(8,128)(2,1)S(1)} %get-tuple-element.48.refs_0_, bf16[1,16,2048]{2,1,0:T(8,128)(2,1)S(1)} %collective-permute-done.8.refs_1_, bf16[1,16,2048]{2,1,0:T(8,128)(2,1)S(1)} %collective-permute-done.9.refs_2_, ...), custom_call_target="tpu_custom_call" | custom-call | tf_op jit(solution)/shard_map/widen/pallas_call | solution.py:512
  (18 shorter events, 0.0 us)
Async XLA Ops:
  1.7 11.6 %collective-permute-start = (bf16[128,2048]{1,0:T(8,128)(2,1)S(1)}, bf16[128,2048]{1,0:T(8,128)(2,1)S(1)}, u32[]{:S(2)}, u32[]{:S(2)}) collective-permute-start(bf16[128,2048]{1,0:T(8,128)(2,1)S(1)} %slice.3), channel_id=1, source_target_pairs={{0,4},{4,8},{8,12},{12,16},{16,20},{20,24},{24,28},{1,5},{5,9},{9,... | collective-permute-start | bytes 1572872 | tf_op jit(solution)/shard_map/ppermute | solution.py:361
  7.4 5.9 %copy-start.2 = (f32[16,2048]{1,0:T(8,128)S(1)}, f32[16,2048]{1,0:T(8,128)}, u32[]{:S(2)}) copy-start(f32[16,2048]{1,0:T(8,128)} %get-tuple-element.33.rates.rest_8_) | copy-start | bytes 393220
  7.5 5.9 %copy-start.5 = (bf16[5,128,128]{2,1,0:T(8,128)(2,1)S(1)}, bf16[5,128,128]{2,1,0:T(8,128)(2,1)}, u32[]{:S(2)}) copy-start(bf16[5,128,128]{2,1,0:T(8,128)(2,1)} %get-tuple-element.30.masks) | copy-start | bytes 491524
  7.5 5.9 %copy-start.6 = (f32[16,2048]{1,0:T(8,128)S(1)}, f32[16,2048]{1,0:T(8,128)}, u32[]{:S(2)}) copy-start(f32[16,2048]{1,0:T(8,128)} %get-tuple-element.34.gains) | copy-start | bytes 393220
  7.5 5.9 %copy-start.8 = (f32[256]{0:T(256)S(1)}, f32[256]{0:T(256)}, u32[]{:S(2)}) copy-start(f32[256]{0:T(256)} %get-tuple-element.27.keep) | copy-start | bytes 3076
  7.5 5.9 %copy-start.11 = (s32[16]{0:T(128)S(1)}, s32[16]{0:T(128)}, u32[]{:S(2)}) copy-start(s32[16]{0:T(128)} %get-tuple-element.28.last) | copy-start | bytes 196
  7.5 20.5 %copy-start.14 = (f32[16,128]{1,0:T(8,128)S(1)}, f32[16,128]{1,0:T(8,128)}, u32[]{:S(2)}) copy-start(f32[16,128]{1,0:T(8,128)} %rates.1) | copy-start | bytes 24580
  7.5 20.7 %copy-start.15 = (f32[16,128]{1,0:T(8,128)S(1)}, f32[16,128]{1,0:T(8,128)}, u32[]{:S(2)}) copy-start(f32[16,128]{1,0:T(8,128)} %resid.1) | copy-start | bytes 24580
  13.3 24.6 %copy-start.9 = (s32[65]{0:T(128)S(1)}, s32[65]{0:T(128)}, u32[]{:S(2)}) copy-start(s32[65]{0:T(128)} %offsets.5) | copy-start | bytes 784
  13.3 24.6 %copy-start.12 = (f32[2048]{0:T(1024)S(1)}, f32[2048]{0:T(1024)}, u32[]{:S(2)}) copy-start(f32[2048]{0:T(1024)} %param.15) | copy-start | bytes 24580
  13.4 1.0 %copy-start.3 = (bf16[128,2048]{1,0:T(8,128)(2,1)S(1)}, bf16[128,2048]{1,0:T(8,128)(2,1)}, u32[]{:S(2)}) copy-start(bf16[128,2048]{1,0:T(8,128)(2,1)} %get-tuple-element.32.second) | copy-start | bytes 1572868
  14.4 23.5 %copy-start.4 = (bf16[128,2048]{1,0:T(8,128)(2,1)S(1)}, bf16[128,2048]{1,0:T(8,128)(2,1)}, u32[]{:S(2)}) copy-start(bf16[128,2048]{1,0:T(8,128)(2,1)} %get-tuple-element.32.second) | copy-start | bytes 1572868
  23.9 6.3 %collective-permute-start.1 = (bf16[3,16,2048]{2,1,0:T(8,128)(2,1)S(1)}, bf16[3,16,2048]{2,1,0:T(8,128)(2,1)S(1)}, u32[]{:S(2)}, u32[]{:S(2)}) collective-permute-start(bf16[3,16,2048]{2,1,0:T(8,128)(2,1)S(1)} %get-tuple-element.39), channel_id=1, source_target_pairs={{0,4},{4,8},{8,12},{12,16},{16,20},{20,24},{24,28},{28,0},{1,5},{5... | collective-permute-start | bytes 589832 | tf_op jit(solution)/shard_map/ppermute | solution.py:447
  26.5 8.3 %collective-permute-start.2 = (bf16[3,16,2048]{2,1,0:T(8,128)(2,1)S(1)}, bf16[3,16,2048]{2,1,0:T(8,128)(2,1)S(1)}, u32[]{:S(2)}, u32[]{:S(2)}) collective-permute-start(bf16[3,16,2048]{2,1,0:T(8,128)(2,1)S(1)} %get-tuple-element.40), channel_id=1, source_target_pairs={{0,8},{4,12},{8,16},{12,20},{16,24},{20,28},{24,0},{28,4},{1,9},{5... | collective-permute-start | bytes 589832 | tf_op jit(solution)/shard_map/ppermute | solution.py:447
  28.4 16.8 %collective-permute-start.3 = (bf16[3,16,2048]{2,1,0:T(8,128)(2,1)S(1)}, bf16[3,16,2048]{2,1,0:T(8,128)(2,1)S(1)}, u32[]{:S(2)}, u32[]{:S(2)}) collective-permute-start(bf16[3,16,2048]{2,1,0:T(8,128)(2,1)S(1)} %get-tuple-element.41), channel_id=1, source_target_pairs={{0,12},{4,16},{8,20},{12,24},{16,28},{20,0},{24,4},{28,8},{1,13},{... | collective-permute-start | bytes 589832 | tf_op jit(solution)/shard_map/ppermute | solution.py:447
  29.3 15.9 %collective-permute-start.4 = (bf16[3,16,2048]{2,1,0:T(8,128)(2,1)S(1)}, bf16[3,16,2048]{2,1,0:T(8,128)(2,1)S(1)}, u32[]{:S(2)}, u32[]{:S(2)}) collective-permute-start(bf16[3,16,2048]{2,1,0:T(8,128)(2,1)S(1)} %get-tuple-element.42), channel_id=1, source_target_pairs={{0,16},{4,20},{8,24},{12,28},{16,0},{20,4},{24,8},{28,12},{1,17},{... | collective-permute-start | bytes 589832 | tf_op jit(solution)/shard_map/ppermute | solution.py:447
  29.8 15.4 %collective-permute-start.5 = (bf16[3,16,2048]{2,1,0:T(8,128)(2,1)S(1)}, bf16[3,16,2048]{2,1,0:T(8,128)(2,1)S(1)}, u32[]{:S(2)}, u32[]{:S(2)}) collective-permute-start(bf16[3,16,2048]{2,1,0:T(8,128)(2,1)S(1)} %get-tuple-element.43), channel_id=1, source_target_pairs={{0,20},{4,24},{8,28},{12,0},{16,4},{20,8},{24,12},{28,16},{1,21},{... | collective-permute-start | bytes 589832 | tf_op jit(solution)/shard_map/ppermute | solution.py:447
  30.2 15.0 %collective-permute-start.6 = (bf16[3,16,2048]{2,1,0:T(8,128)(2,1)S(1)}, bf16[3,16,2048]{2,1,0:T(8,128)(2,1)S(1)}, u32[]{:S(2)}, u32[]{:S(2)}) collective-permute-start(bf16[3,16,2048]{2,1,0:T(8,128)(2,1)S(1)} %get-tuple-element.44), channel_id=1, source_target_pairs={{0,24},{4,28},{8,0},{12,4},{16,8},{20,12},{24,16},{28,20},{1,25},{... | collective-permute-start | bytes 589832 | tf_op jit(solution)/shard_map/ppermute | solution.py:447
  34.8 10.5 %collective-permute-start.7 = (bf16[3,16,2048]{2,1,0:T(8,128)(2,1)S(1)}, bf16[3,16,2048]{2,1,0:T(8,128)(2,1)S(1)}, u32[]{:S(2)}, u32[]{:S(2)}) collective-permute-start(bf16[3,16,2048]{2,1,0:T(8,128)(2,1)S(1)} %get-tuple-element.45), channel_id=1, source_target_pairs={{0,28},{4,0},{8,4},{12,8},{16,12},{20,16},{24,20},{28,24},{1,29},{... | collective-permute-start | bytes 589832 | tf_op jit(solution)/shard_map/ppermute | solution.py:447
  37.9 0.9 %copy-start.13 = (f32[2,128,128]{2,1,0:T(8,128)S(1)}, f32[2,128,128]{2,1,0:T(8,128)}, u32[]{:S(2)}) copy-start(f32[2,128,128]{2,1,0:T(8,128)} %get-tuple-element.36.taps) | copy-start | bytes 393220
  38.8 6.5 %copy-start.10 = (s32[32]{0:T(128)S(1)}, s32[32]{0:T(128)}, u32[]{:S(2)}) copy-start(s32[32]{0:T(128)} %owners.3) | copy-start | bytes 388
  44.2 1.0 %copy-start.1 = (bf16[256,2048]{1,0:T(8,128)(2,1)}, bf16[256,2048]{1,0:T(8,128)(2,1)S(1)}, u32[]{:S(2)}) copy-start(bf16[256,2048]{1,0:T(8,128)(2,1)S(1)} %get-tuple-element.47.weight) | copy-start | bytes 3145732
  45.2 7.6 %copy-start = (bf16[256,2048]{1,0:T(8,128)(2,1)}, bf16[256,2048]{1,0:T(8,128)(2,1)S(1)}, u32[]{:S(2)}) copy-start(bf16[256,2048]{1,0:T(8,128)(2,1)S(1)} %get-tuple-element.37.rest_9_.local) | copy-start | bytes 3145732
  47.5 0.7 %copy-start.7 = (f32[16,2048]{1,0:T(8,128)}, f32[16,2048]{1,0:T(8,128)S(1)}, u32[]{:S(2)}) copy-start(f32[16,2048]{1,0:T(8,128)S(1)} %get-tuple-element.46.entering) | copy-start | bytes 393220
  48.2 7.7 %collective-permute-start.10 = (bf16[1,16,2048]{2,1,0:T(8,128)(2,1)S(1)}, bf16[1,16,2048]{2,1,0:T(8,128)(2,1)S(1)}, u32[]{:S(2)}, u32[]{:S(2)}) collective-permute-start(bf16[1,16,2048]{2,1,0:T(8,128)(2,1)S(1)} %get-tuple-element.51), channel_id=1, source_target_pairs={{0,3},{1,0},{2,1},{3,2},{4,7},{5,4},{6,5},{7,6},{8,11},{9,8},{10,9... | collective-permute-start | bytes 196616 | tf_op jit(solution)/shard_map/ppermute | solution.py:496
  51.8 6.8 %collective-permute-start.8 = (bf16[1,16,2048]{2,1,0:T(8,128)(2,1)S(1)}, bf16[1,16,2048]{2,1,0:T(8,128)(2,1)S(1)}, u32[]{:S(2)}, u32[]{:S(2)}) collective-permute-start(bf16[1,16,2048]{2,1,0:T(8,128)(2,1)S(1)} %get-tuple-element.49), channel_id=1, source_target_pairs={{0,1},{1,2},{2,3},{3,0},{4,5},{5,6},{6,7},{7,4},{8,9},{9,10},{10,1... | collective-permute-start | bytes 196616 | tf_op jit(solution)/shard_map/ppermute | solution.py:496
  51.8 8.0 %collective-permute-start.9 = (bf16[1,16,2048]{2,1,0:T(8,128)(2,1)S(1)}, bf16[1,16,2048]{2,1,0:T(8,128)(2,1)S(1)}, u32[]{:S(2)}, u32[]{:S(2)}) collective-permute-start(bf16[1,16,2048]{2,1,0:T(8,128)(2,1)S(1)} %get-tuple-element.50), channel_id=1, source_target_pairs={{0,2},{1,3},{2,0},{3,1},{4,6},{5,7},{6,4},{7,5},{8,10},{9,11},{10,... | collective-permute-start | bytes 196616 | tf_op jit(solution)/shard_map/ppermute | solution.py:496

commit v2 on v1

--- a/solution.py
+++ b/solution.py
@@ -10,7 +10,8 @@
 TAPS = 128
 ENDS = 16
 LANES = 128
-BLOCK = 512
+BLOCK = 1024
+PART = 512
 CHUNK = 16
 F32 = jnp.float32
 BF16 = jnp.bfloat16
@@ -172,15 +173,16 @@
         gains_out[:, at] = gain(wide)
 
 
-def second_kernel(size, value, key, rows, masks, mixed_out, circulants):
+def second_kernel(size, value, key, rows, masks, kept):
     per_tile = LANES // size
-    for tile in range(value.shape[1] // LANES):
+    tiles = value.shape[1] // LANES
+    for tile in range(tiles):
         at = slice(tile * LANES, (tile + 1) * LANES)
         blocks = []
         for g in range(tile * per_tile, (tile + 1) * per_tile):
             blocks.append(circulant(rows[g : g + 1]))
-            circulants[g] = blocks[-1]
-        mixed_out[:, at] = filtered(blocks, masks, 2, 3, value[:, at], key[:, at])
+            kept[g] = blocks[-1]
+        kept[tiles * per_tile + tile] = filtered(blocks, masks, 2, 3, value[:, at], key[:, at])
 
 
 def states_kernel(
@@ -192,9 +194,8 @@
     halo,
     value,
     key,
-    circulants,
+    kept,
     masks,
-    second,
     rates,
     gains,
     mixed_out,
@@ -211,16 +212,19 @@
         at = slice(tile * LANES, (tile + 1) * LANES)
         spot = pl.ds(pl.multiple_of(step * block + tile * LANES, LANES), LANES)
         window = jnp.concatenate([halo[:, at], value[:, at]], axis=0)
-        blocks = [circulants[tile * per_tile + g] for g in range(per_tile)]
+        blocks = [kept[tile * per_tile + g] for g in range(per_tile)]
+        second = kept[block // LANES * per_tile + tile]
         mixed = filtered(blocks, masks, 0, 1, window, key[:, at])
-        mixed_out[:, at] = mixed
+        mixed_out[:TAPS, at] = mixed
+        mixed_out[TAPS:, at] = second
         wide[:TAPS, spot] = mixed.astype(F32)
-        wide[TAPS:, spot] = second[:, at].astype(F32)
+        wide[TAPS:, spot] = second.astype(F32)
 
     @pl.when(step == pl.num_programs(0) - 1)
     def run():
-        for first in range(0, width, block):
-            lanes = slice(first, first + block)
+        part = history.shape[2]
+        for first in range(0, width, part):
+            lanes = slice(first, first + part)
             fade = jnp.exp(-rates[:, lanes])
 
             def some(c, state):
@@ -230,7 +234,7 @@
                     history[base + t] = state
                 return state
 
-            state = lax.fori_loop(0, length // CHUNK, some, jnp.zeros((poles, block), F32))
+            state = lax.fori_loop(0, length // CHUNK, some, jnp.zeros((poles, part), F32))
             scale = gains[:, lanes]
             through = (state * scale).astype(BF16)
             for d in range(peers):
@@ -242,9 +246,9 @@
 
 
 def local_kernel(
-    size, offsets, place, first, second, masks, taps, skip, rates, resid, local_out, weight_out, limit
+    size, offsets, place, mixed, masks, taps, skip, rates, resid, local_out, weight_out, limit
 ):
-    length, block = 2 * TAPS, first.shape[1]
+    length, block = mixed.shape
     begin = place[0] * length
     step = pl.program_id(0)
     per_tile = LANES // size
@@ -258,7 +262,7 @@
     lane_group = iota((TAPS, LANES), 1) // size
     for tile in range(block // LANES):
         at = slice(tile * LANES, (tile + 1) * LANES)
-        x = jnp.concatenate([first[:, at], second[:, at]], axis=0)
+        x = mixed[:, at]
         acc0 = jnp.zeros((TAPS, LANES), F32)
         acc1 = jnp.zeros((TAPS, LANES), F32)
         for g in range(per_tile):
@@ -290,7 +294,7 @@
     spans = []
     for d in range(lines):
         for q in range(per_line):
-            k = lax.rem(line[0] + d, lines) * per_line + q
+            k = (line[0] ^ d) * per_line + q
             doc = owners[me * (lines * per_line) + k]
             start, end = offsets[doc], offsets[doc + 1] - 1
             spot = d * per_line + q
@@ -342,7 +346,7 @@
     parts, out = refs[:-1], refs[-1]
     width = parts[0].shape[2]
     for d, part in enumerate(parts):
-        source = lax.rem(line[0] - d + len(parts), len(parts))
+        source = line[0] ^ d
         out[:, :, pl.ds(pl.multiple_of(source * width, width), width)] = part[...].astype(F32)
 
 
@@ -393,7 +397,8 @@
     def half(row, size=block):
         return pl.BlockSpec((TAPS, size), lambda i: (row, i))
 
-    second, circulants = pl.pallas_call(
+    entries = block // size + block // LANES
+    kept = pl.pallas_call(
         functools.partial(second_kernel, size),
         grid=(width // block,),
         in_specs=[
@@ -402,11 +407,8 @@
             pl.BlockSpec((block // size, TAPS), lambda i: (i, 0)),
             whole((5, TAPS, TAPS)),
         ],
-        out_specs=[half(0), pl.BlockSpec((block // size, TAPS, TAPS), lambda i: (i, 0, 0))],
-        out_shape=[
-            jax.ShapeDtypeStruct((TAPS, width), BF16),
-            jax.ShapeDtypeStruct((groups, TAPS, TAPS), BF16),
-        ],
+        out_specs=pl.BlockSpec((entries, TAPS, TAPS), lambda i: (i, 0, 0)),
+        out_shape=jax.ShapeDtypeStruct((width // block * entries, TAPS, TAPS), BF16),
         compiler_params=params(1, 60),
         cost_estimate=pl.CostEstimate(
             flops=16 * length * length * width, bytes_accessed=7 * length * width, transcendentals=0
@@ -414,7 +416,7 @@
         name="second",
     )(value, key, rows, masks)
 
-    first, *ends = pl.pallas_call(
+    mixed, *ends = pl.pallas_call(
         functools.partial(states_kernel, cap, size),
         grid=(width // block,),
         in_specs=[
@@ -424,22 +426,21 @@
             half(0),
             half(0),
             half(0),
-            pl.BlockSpec((block // size, TAPS, TAPS), lambda i: (i, 0, 0)),
+            pl.BlockSpec((entries, TAPS, TAPS), lambda i: (i, 0, 0)),
             whole((5, TAPS, TAPS)),
-            half(0),
             whole((poles, width)),
             whole((poles, width)),
         ],
-        out_specs=[half(0)] + [whole((cap + 1, poles, width))] * peers,
-        out_shape=[jax.ShapeDtypeStruct((TAPS, width), BF16)]
+        out_specs=[lanes(length)] + [whole((cap + 1, poles, width))] * peers,
+        out_shape=[jax.ShapeDtypeStruct((length, width), BF16)]
         + [jax.ShapeDtypeStruct((cap + 1, poles, width), BF16)] * peers,
         scratch_shapes=[
             pltpu.VMEM((length, width), F32),
-            pltpu.VMEM((length, poles, block), F32),
+            pltpu.VMEM((length, poles, min(block, PART)), F32),
         ],
         compiler_params=params(1, 50),
         name="states",
-    )(place, keep, last, halo, value, key, circulants, masks, second, rates_wide, gains_wide)
+    )(place, keep, last, halo, value, key, kept, masks, rates_wide, gains_wide)
 
     got = [ends[0]]
     for d in range(1, peers):
@@ -453,8 +454,7 @@
         in_specs=[
             SMEM,
             SMEM,
-            half(0, broad),
-            half(0, broad),
+            lanes(length, broad),
             whole((5, TAPS, TAPS)),
             pl.BlockSpec((2, broad // size, TAPS), lambda i: (0, i, 0)),
             lanes(1, broad),
@@ -472,7 +472,7 @@
             flops=32 * length * length * width, bytes_accessed=6 * length * width, transcendentals=0
         ),
         name="local",
-    )(offsets, place, first, second, masks, taps, skip.reshape(1, width), rates_flat, resid_flat)
+    )(offsets, place, mixed, masks, taps, skip.reshape(1, width), rates_flat, resid_flat)
 
     per_line = slots // lines
     entering, *picked = pl.pallas_call(
@@ -492,7 +492,7 @@
 
     arrived = [picked[0]]
     for d in range(1, lines):
-        route = [(i, (i + d) % lines) for i in range(lines)]
+        route = [(i, i ^ d) for i in range(lines)]
         arrived.append(lax.ppermute(picked[d], "ch", route))
 
     thin = min(width, 8 * LANES)
@@ -502,7 +502,7 @@
         in_specs=[lanes(length, thin), lanes(length, thin), lanes(poles, thin), lanes(length, thin)],
         out_specs=lanes(length, thin),
         out_shape=jax.ShapeDtypeStruct((length, width), BF16),
-        compiler_params=params(1, 60),
+        compiler_params=params(1, 52),
         cost_estimate=pl.CostEstimate(
             flops=3 * 512 * length * width, bytes_accessed=12 * length * width, transcendentals=0
         ),

time: 61.4 us -> 57.5 us (0.936)
  local copies, waits for them, and re-layouts: 5.06 us -> 3.37 us
  Pallas kernels: 30.1 us -> 29.1 us
    unnamed x32 -> x28, local copies, waits for them, and re-layouts: 3.6 us -> 1.91 us
  transfers between devices with their start and end apart: 11 -> 11, of which waited for: 3 -> 3; matrix products, arithmetic and copies ran while one was open for 1% -> 1% of each run, Pallas kernels for 29% -> 30%
where the time goes in v2:
time: 57.5 us; the launch traced here: 57.2 us
  Pallas kernels  29.1 us (51%)
  starting transfers between devices  19.6 us (34%)
  waiting for transfers between devices  4.21 us (7%)
  local copies, waits for them, and re-layouts  3.37 us (6%)
  between operations  0.85 us (1%)
    ppermute x7, starting transfers between devices, per_device(): got.append(lax.ppermute(ends[d], 'ctx', route))  12.8 us
    pallas_call x1, Pallas kernels, per_device(): pl.pallas_call(functools.partial(states_kernel, cap, size), grid=(width /...  8.99 us
    pallas_call x1, Pallas kernels, per_device(): pl.pallas_call(functools.partial(second_kernel, size), grid=(width // blo...  5.47 us
    pallas_call x1, Pallas kernels, per_device(): pl.pallas_call(functools.partial(local_kernel, size), grid=(width // broa...  5.46 us
    ppermute x3, starting transfers between devices, per_device(): arrived.append(lax.ppermute(picked[d], 'ch', route))  4.45 us
    ppermute x3, waiting for transfers between devices, per_device(): arrived.append(lax.ppermute(picked[d], 'ch', route))  3.36 us
    pallas_call x1, Pallas kernels, per_device(): pl.pallas_call(functools.partial(prepare_kernel, cap, peers, size), in_sp...  3.34 us
    pallas_call x1, Pallas kernels, per_device(): pl.pallas_call(functools.partial(output_kernel, size), grid=(width // thi...  2.75 us
  transfers between devices with their start and end apart: 11, of which 3 were waited for; matrix products, arithmetic and copies ran while one was open for 1% of the time, Pallas kernels for 30%

profile of v2, /device:TPU:0, one launch (start us, length us, event | category | flops | bytes accessed | tf_op | source)
XLA Modules:
  0.0 57.2 jit_solution(17434293915186099916)
XLA Ops:
  0.6 1.1 %slice.3 = bf16[128,2048]{1,0:T(8,128)(2,1)S(1)} slice(bf16[256,2048]{1,0:T(8,128)(2,1)} %value.3), slice={[128:256], [0:2048]} | slice | bytes 1048576 | tf_op jit(solution)/shard_map/slice | solution.py:366
  1.7 2.4 %collective-permute-start = (bf16[128,2048]{1,0:T(8,128)(2,1)S(1)}, bf16[128,2048]{1,0:T(8,128)(2,1)S(1)}, u32[]{:S(2)}, u32[]{:S(2)}) collective-permute-start(bf16[128,2048]{1,0:T(8,128)(2,1)S(1)} %slice.3), channel_id=1, source_target_pairs={{0,4},{4,8},{8,12},{12,16},{16,20},{20,24},{24,28},{1,5},{5,9},{9,... | collective-permute-start | bytes 1572872 | tf_op jit(solution)/shard_map/ppermute | solution.py:365
  4.1 3.3 %prepare.1 = (f32[16,2048]{1,0:T(8,128)}, f32[16,2048]{1,0:T(8,128)}, f32[128,128]{1,0:T(8,128)}, bf16[5,128,128]{2,1,0:T(8,128)(2,1)}, f32[2,128,128]{2,1,0:T(8,128)}, /*index=5*/f32[256]{0:T(256)}, s32[16]{0:T(128)}) custom-call(s32[65]{0:T(128)} %offsets.5, s32[32]{0:T(128)} %owners.3, s32[1]{0:T(128)} %bitcast.place, bf16[128,128]{1,0:T(8,128)(2,1)} %filt.1, ...), custom_call_target="tpu_custom_call" | custom-call | flops 1073741824 | bytes 1048576 | tf_op jit(solution)/shard_map/prepare/pallas_call | solution.py:379
  7.5 0.0 copy-start.3
  7.5 0.0 copy-start.4
  7.5 0.0 copy-start.5
  7.5 0.0 copy-start.6
  7.5 0.0 copy-start.9
  7.5 5.5 %second.1.kept = bf16[144,128,128]{2,1,0:T(8,128)(2,1)} custom-call(bf16[256,2048]{1,0:T(8,128)(2,1)} %value.3, bf16[256,2048]{1,0:T(8,128)(2,1)} %key.3, f32[128,128]{1,0:T(8,128)} %get-tuple-element.27.rows, bf16[5,128,128]{2,1,0:T(8,128)(2,1)} %get-tuple-element.28.masks), custom_call_target="tpu_custom_call" | custom-call | flops 2147483648 | bytes 3670016 | tf_op jit(solution)/shard_map/second/pallas_call | solution.py:401
  13.0 0.0 copy-start.10
  13.0 0.0 collective-permute-done.halo
  13.0 0.0 copy-done.3
  13.0 0.0 copy-done.4
  13.0 0.0 copy-done.5
  13.1 0.0 copy-done.6
  13.1 0.0 copy-done.9
  13.1 9.0 %states.1 = (bf16[256,2048]{1,0:T(8,128)(2,1)S(1)}, bf16[3,16,2048]{2,1,0:T(8,128)(2,1)S(1)}, bf16[3,16,2048]{2,1,0:T(8,128)(2,1)S(1)}, bf16[3,16,2048]{2,1,0:T(...) custom-call(s32[1]{0:T(128)} %bitcast.place, ...), custom_call_target="tpu_custom_call" | custom-call | tf_op jit(solution)/shard_map/states/pallas_call | solution.py:419
  22.1 2.6 %collective-permute-start.1 = (bf16[3,16,2048]{2,1,0:T(8,128)(2,1)S(1)}, bf16[3,16,2048]{2,1,0:T(8,128)(2,1)S(1)}, u32[]{:S(2)}, u32[]{:S(2)}) collective-permute-start(bf16[3,16,2048]{2,1,0:T(8,128)(2,1)S(1)} %get-tuple-element.35), channel_id=1, source_target_pairs={{0,4},{4,8},{8,12},{12,16},{16,20},{20,24},{24,28},{28,0},{1,5},{5... | collective-permute-start | bytes 589832 | tf_op jit(solution)/shard_map/ppermute | solution.py:448
  24.7 1.5 %collective-permute-start.2 = (bf16[3,16,2048]{2,1,0:T(8,128)(2,1)S(1)}, bf16[3,16,2048]{2,1,0:T(8,128)(2,1)S(1)}, u32[]{:S(2)}, u32[]{:S(2)}) collective-permute-start(bf16[3,16,2048]{2,1,0:T(8,128)(2,1)S(1)} %get-tuple-element.36), channel_id=1, source_target_pairs={{0,8},{4,12},{8,16},{12,20},{16,24},{20,28},{24,0},{28,4},{1,9},{5... | collective-permute-start | bytes 589832 | tf_op jit(solution)/shard_map/ppermute | solution.py:448
  26.2 0.1 copy.13
  26.3 0.1 reshape.21.rates
  26.4 0.0 copy-done.13
  26.4 0.1 copy.14
  26.5 0.1 reshape.22.resid
  26.6 0.9 %collective-permute-start.3 = (bf16[3,16,2048]{2,1,0:T(8,128)(2,1)S(1)}, bf16[3,16,2048]{2,1,0:T(8,128)(2,1)S(1)}, u32[]{:S(2)}, u32[]{:S(2)}) collective-permute-start(bf16[3,16,2048]{2,1,0:T(8,128)(2,1)S(1)} %get-tuple-element.37), channel_id=1, source_target_pairs={{0,12},{4,16},{8,20},{12,24},{16,28},{20,0},{24,4},{28,8},{1,13},{... | collective-permute-start | bytes 589832 | tf_op jit(solution)/shard_map/ppermute | solution.py:448
  27.5 0.5 collective-permute-start.4
  28.0 0.4 collective-permute-start.5
  28.4 0.0 collective-permute-done.1.rest_1_
  28.4 3.7 %collective-permute-start.6 = (bf16[3,16,2048]{2,1,0:T(8,128)(2,1)S(1)}, bf16[3,16,2048]{2,1,0:T(8,128)(2,1)S(1)}, u32[]{:S(2)}, u32[]{:S(2)}) collective-permute-start(bf16[3,16,2048]{2,1,0:T(8,128)(2,1)S(1)} %get-tuple-element.40), channel_id=1, source_target_pairs={{0,24},{4,28},{8,0},{12,4},{16,8},{20,12},{24,16},{28,20},{1,25},{... | collective-permute-start | bytes 589832 | tf_op jit(solution)/shard_map/ppermute | solution.py:448
  32.2 0.8 %collective-permute-done.2.rest_2_ = bf16[3,16,2048]{2,1,0:T(8,128)(2,1)S(1)} collective-permute-done((bf16[3,16,2048]{2,1,0:T(8,128)(2,1)S(1)}, bf16[3,16,2048]{2,1,0:T(8,128)(2,1)S(1)}, u32[]{:S(2)}, u32[]{:S(2)}) %collective-permute-start.2) | collective-permute-done | bytes 196640 | tf_op jit(solution)/shard_map/ppermute | solution.py:448
  33.0 3.1 %collective-permute-start.7 = (bf16[3,16,2048]{2,1,0:T(8,128)(2,1)S(1)}, bf16[3,16,2048]{2,1,0:T(8,128)(2,1)S(1)}, u32[]{:S(2)}, u32[]{:S(2)}) collective-permute-start(bf16[3,16,2048]{2,1,0:T(8,128)(2,1)S(1)} %get-tuple-element.41), channel_id=1, source_target_pairs={{0,28},{4,0},{8,4},{12,8},{16,12},{20,16},{24,20},{28,24},{1,29},{... | collective-permute-start | bytes 589832 | tf_op jit(solution)/shard_map/ppermute | solution.py:448
  36.1 0.9 %copy-done.11 = f32[2,128,128]{2,1,0:T(8,128)S(1)} copy-done((f32[2,128,128]{2,1,0:T(8,128)S(1)}, f32[2,128,128]{2,1,0:T(8,128)}, u32[]{:S(2)}) %copy-start.11) | copy-done | bytes 131096
  37.0 5.5 %local.1 = (bf16[256,2048]{1,0:T(8,128)(2,1)S(1)}, bf16[256,2048]{1,0:T(8,128)(2,1)S(1)}) custom-call(s32[65]{0:T(128)S(1)} %copy-done.7, s32[1]{0:T(128)} %bitcast.place, bf16[256,2048]{1,0:T(8,128)(2,1)S(1)} %get-tuple-element.31.mixed, bf16[5,128,128]{2,1,0:T(8,128)(2,1)S(1)} %copy-done.4, f32[2,128,128]{2,1,0:T(8,128)S(1)} %copy-done.11, ...), custom_call_target="tpu_custom_call" | custom-call | flops 4294967296 | bytes 3145728 | tf_op jit(solution)/shard_map/local/pallas_call | solution.py:451
  42.5 0.9 %copy-done.2 = bf16[256,2048]{1,0:T(8,128)(2,1)} copy-done((bf16[256,2048]{1,0:T(8,128)(2,1)}, bf16[256,2048]{1,0:T(8,128)(2,1)S(1)}, u32[]{:S(2)}) %copy-start.2) | copy-done | bytes 1048600
  43.4 0.0 collective-permute-done.3.rest_3_
  43.4 0.0 collective-permute-done.4.rest_4_
  43.4 0.0 collective-permute-done.5.rest_5_
  43.5 0.0 collective-permute-done.6.rest_6_
  43.5 0.0 collective-permute-done.7.rest_7_
  43.5 2.3 %slots.1 = (f32[16,2048]{1,0:T(8,128)S(1)}, bf16[1,16,2048]{2,1,0:T(8,128)(2,1)S(1)}, bf16[1,16,2048]{2,1,0:T(8,128)(2,1)S(1)}, bf16[1,16,2048]{2,1,0:T(8,128)(2,1)S(1)}, bf16[1,16,2048]{2,1,0:T(8,128)(2,1)S(1)}) custom-call(s32[65]{0:T(128)S(1)} %copy-done.7, s32[32]{0:T(128)S(1)} %copy-done.8, s32[1]{0:T(128)} %bitcast.place, s32[1]{0:T(128)} %bitcast.4.line, ...), custom_call_target="tpu_custom_call" | custom-call | tf_op jit(solution)/shard_map/slots/pallas_call | solution.py:478
  45.8 3.6 %collective-permute-start.10 = (bf16[1,16,2048]{2,1,0:T(8,128)(2,1)S(1)}, bf16[1,16,2048]{2,1,0:T(8,128)(2,1)S(1)}, u32[]{:S(2)}, u32[]{:S(2)}) collective-permute-start(bf16[1,16,2048]{2,1,0:T(8,128)(2,1)S(1)} %get-tuple-element.47), channel_id=1, source_target_pairs={{0,3},{1,2},{2,1},{3,0},{4,7},{5,6},{6,5},{7,4},{8,11},{9,10},{10,... | collective-permute-start | bytes 196616 | tf_op jit(solution)/shard_map/ppermute | solution.py:496
  49.4 0.0 collective-permute-start.8
  49.4 0.8 %collective-permute-start.9 = (bf16[1,16,2048]{2,1,0:T(8,128)(2,1)S(1)}, bf16[1,16,2048]{2,1,0:T(8,128)(2,1)S(1)}, u32[]{:S(2)}, u32[]{:S(2)}) collective-permute-start(bf16[1,16,2048]{2,1,0:T(8,128)(2,1)S(1)} %get-tuple-element.46), channel_id=1, source_target_pairs={{0,2},{1,3},{2,0},{3,1},{4,6},{5,7},{6,4},{7,5},{8,10},{9,11},{10,... | collective-permute-start | bytes 196616 | tf_op jit(solution)/shard_map/ppermute | solution.py:496
  50.2 2.7 %output.1 = bf16[256,2048]{1,0:T(8,128)(2,1)} custom-call(bf16[256,2048]{1,0:T(8,128)(2,1)S(1)} %copy-done.1, bf16[256,2048]{1,0:T(8,128)(2,1)} %copy-done, f32[16,2048]{1,0:T(8,128)S(1)} %get-tuple-element.42.entering, bf16[256,2048]{1,0:T(8,128)(2,1)} %copy-done.2), custom_call_target="tpu_custom_call" | custom-call | flops 805306368 | bytes 6291456 | tf_op jit(solution)/shard_map/output/pallas_call | solution.py:499
  53.0 0.0 collective-permute-done.10.refs_3_
  53.0 2.3 %collective-permute-done.8.refs_1_ = bf16[1,16,2048]{2,1,0:T(8,128)(2,1)S(1)} collective-permute-done((bf16[1,16,2048]{2,1,0:T(8,128)(2,1)S(1)}, bf16[1,16,2048]{2,1,0:T(8,128)(2,1)S(1)}, u32[]{:S(2)}, u32[]{:S(2)}) %collective-permute-start.8) | collective-permute-done | bytes 65568 | tf_op jit(solution)/shard_map/ppermute | solution.py:496
  55.3 1.1 %collective-permute-done.9.refs_2_ = bf16[1,16,2048]{2,1,0:T(8,128)(2,1)S(1)} collective-permute-done((bf16[1,16,2048]{2,1,0:T(8,128)(2,1)S(1)}, bf16[1,16,2048]{2,1,0:T(8,128)(2,1)S(1)}, u32[]{:S(2)}, u32[]{:S(2)}) %collective-permute-start.9) | collective-permute-done | bytes 65568 | tf_op jit(solution)/shard_map/ppermute | solution.py:496
  56.3 0.8 %widen.1 = f32[1,16,8192]{2,1,0:T(8,128)} custom-call(s32[1]{0:T(128)} %bitcast.4.line, bf16[1,16,2048]{2,1,0:T(8,128)(2,1)S(1)} %get-tuple-element.44.refs_0_, bf16[1,16,2048]{2,1,0:T(8,128)(2,1)S(1)} %collective-permute-done.8.refs_1_, bf16[1,16,2048]{2,1,0:T(8,128)(2,1)S(1)} %collective-permute-done.9.refs_2_, ...), custom_call_target="tpu_custom_call" | custom-call | tf_op jit(solution)/shard_map/widen/pallas_call | solution.py:512
  (14 shorter events, 0.0 us)
Async XLA Ops:
  1.7 11.3 %collective-permute-start = (bf16[128,2048]{1,0:T(8,128)(2,1)S(1)}, bf16[128,2048]{1,0:T(8,128)(2,1)S(1)}, u32[]{:S(2)}, u32[]{:S(2)}) collective-permute-start(bf16[128,2048]{1,0:T(8,128)(2,1)S(1)} %slice.3), channel_id=1, source_target_pairs={{0,4},{4,8},{8,12},{12,16},{16,20},{20,24},{24,28},{1,5},{5,9},{9,... | collective-permute-start | bytes 1572872 | tf_op jit(solution)/shard_map/ppermute | solution.py:365
  7.5 5.6 %copy-start.3 = (f32[16,2048]{1,0:T(8,128)S(1)}, f32[16,2048]{1,0:T(8,128)}, u32[]{:S(2)}) copy-start(f32[16,2048]{1,0:T(8,128)} %get-tuple-element.29.rates.rest_8_) | copy-start | bytes 393220
  7.5 5.6 %copy-start.4 = (bf16[5,128,128]{2,1,0:T(8,128)(2,1)S(1)}, bf16[5,128,128]{2,1,0:T(8,128)(2,1)}, u32[]{:S(2)}) copy-start(bf16[5,128,128]{2,1,0:T(8,128)(2,1)} %get-tuple-element.28.masks) | copy-start | bytes 491524
  7.5 5.6 %copy-start.5 = (f32[16,2048]{1,0:T(8,128)S(1)}, f32[16,2048]{1,0:T(8,128)}, u32[]{:S(2)}) copy-start(f32[16,2048]{1,0:T(8,128)} %get-tuple-element.30.gains) | copy-start | bytes 393220
  7.5 5.6 %copy-start.6 = (f32[256]{0:T(256)S(1)}, f32[256]{0:T(256)}, u32[]{:S(2)}) copy-start(f32[256]{0:T(256)} %get-tuple-element.25.keep) | copy-start | bytes 3076
  7.5 5.6 %copy-start.9 = (s32[16]{0:T(128)S(1)}, s32[16]{0:T(128)}, u32[]{:S(2)}) copy-start(s32[16]{0:T(128)} %get-tuple-element.26.last) | copy-start | bytes 196
  13.0 13.2 %copy-start.12 = (f32[16,128]{1,0:T(8,128)S(1)}, f32[16,128]{1,0:T(8,128)}, u32[]{:S(2)}) copy-start(f32[16,128]{1,0:T(8,128)} %rates.1) | copy-start | bytes 24580
  13.0 13.4 %copy-start.13 = (f32[16,128]{1,0:T(8,128)S(1)}, f32[16,128]{1,0:T(8,128)}, u32[]{:S(2)}) copy-start(f32[16,128]{1,0:T(8,128)} %resid.1) | copy-start | bytes 24580
  13.0 23.1 %copy-start.7 = (s32[65]{0:T(128)S(1)}, s32[65]{0:T(128)}, u32[]{:S(2)}) copy-start(s32[65]{0:T(128)} %offsets.5) | copy-start | bytes 784
  13.0 23.1 %copy-start.10 = (f32[2048]{0:T(1024)S(1)}, f32[2048]{0:T(1024)}, u32[]{:S(2)}) copy-start(f32[2048]{0:T(1024)} %param.15) | copy-start | bytes 24580
  22.1 6.4 %collective-permute-start.1 = (bf16[3,16,2048]{2,1,0:T(8,128)(2,1)S(1)}, bf16[3,16,2048]{2,1,0:T(8,128)(2,1)S(1)}, u32[]{:S(2)}, u32[]{:S(2)}) collective-permute-start(bf16[3,16,2048]{2,1,0:T(8,128)(2,1)S(1)} %get-tuple-element.35), channel_id=1, source_target_pairs={{0,4},{4,8},{8,12},{12,16},{16,20},{20,24},{24,28},{28,0},{1,5},{5... | collective-permute-start | bytes 589832 | tf_op jit(solution)/shard_map/ppermute | solution.py:448
  24.7 8.3 %collective-permute-start.2 = (bf16[3,16,2048]{2,1,0:T(8,128)(2,1)S(1)}, bf16[3,16,2048]{2,1,0:T(8,128)(2,1)S(1)}, u32[]{:S(2)}, u32[]{:S(2)}) collective-permute-start(bf16[3,16,2048]{2,1,0:T(8,128)(2,1)S(1)} %get-tuple-element.36), channel_id=1, source_target_pairs={{0,8},{4,12},{8,16},{12,20},{16,24},{20,28},{24,0},{28,4},{1,9},{5... | collective-permute-start | bytes 589832 | tf_op jit(solution)/shard_map/ppermute | solution.py:448
  26.6 16.8 %collective-permute-start.3 = (bf16[3,16,2048]{2,1,0:T(8,128)(2,1)S(1)}, bf16[3,16,2048]{2,1,0:T(8,128)(2,1)S(1)}, u32[]{:S(2)}, u32[]{:S(2)}) collective-permute-start(bf16[3,16,2048]{2,1,0:T(8,128)(2,1)S(1)} %get-tuple-element.37), channel_id=1, source_target_pairs={{0,12},{4,16},{8,20},{12,24},{16,28},{20,0},{24,4},{28,8},{1,13},{... | collective-permute-start | bytes 589832 | tf_op jit(solution)/shard_map/ppermute | solution.py:448
  27.5 15.9 %collective-permute-start.4 = (bf16[3,16,2048]{2,1,0:T(8,128)(2,1)S(1)}, bf16[3,16,2048]{2,1,0:T(8,128)(2,1)S(1)}, u32[]{:S(2)}, u32[]{:S(2)}) collective-permute-start(bf16[3,16,2048]{2,1,0:T(8,128)(2,1)S(1)} %get-tuple-element.38), channel_id=1, source_target_pairs={{0,16},{4,20},{8,24},{12,28},{16,0},{20,4},{24,8},{28,12},{1,17},{... | collective-permute-start | bytes 589832 | tf_op jit(solution)/shard_map/ppermute | solution.py:448
  28.0 15.4 %collective-permute-start.5 = (bf16[3,16,2048]{2,1,0:T(8,128)(2,1)S(1)}, bf16[3,16,2048]{2,1,0:T(8,128)(2,1)S(1)}, u32[]{:S(2)}, u32[]{:S(2)}) collective-permute-start(bf16[3,16,2048]{2,1,0:T(8,128)(2,1)S(1)} %get-tuple-element.39), channel_id=1, source_target_pairs={{0,20},{4,24},{8,28},{12,0},{16,4},{20,8},{24,12},{28,16},{1,21},{... | collective-permute-start | bytes 589832 | tf_op jit(solution)/shard_map/ppermute | solution.py:448
  28.4 15.0 %collective-permute-start.6 = (bf16[3,16,2048]{2,1,0:T(8,128)(2,1)S(1)}, bf16[3,16,2048]{2,1,0:T(8,128)(2,1)S(1)}, u32[]{:S(2)}, u32[]{:S(2)}) collective-permute-start(bf16[3,16,2048]{2,1,0:T(8,128)(2,1)S(1)} %get-tuple-element.40), channel_id=1, source_target_pairs={{0,24},{4,28},{8,0},{12,4},{16,8},{20,12},{24,16},{28,20},{1,25},{... | collective-permute-start | bytes 589832 | tf_op jit(solution)/shard_map/ppermute | solution.py:448
  33.0 10.5 %collective-permute-start.7 = (bf16[3,16,2048]{2,1,0:T(8,128)(2,1)S(1)}, bf16[3,16,2048]{2,1,0:T(8,128)(2,1)S(1)}, u32[]{:S(2)}, u32[]{:S(2)}) collective-permute-start(bf16[3,16,2048]{2,1,0:T(8,128)(2,1)S(1)} %get-tuple-element.41), channel_id=1, source_target_pairs={{0,28},{4,0},{8,4},{12,8},{16,12},{20,16},{24,20},{28,24},{1,29},{... | collective-permute-start | bytes 589832 | tf_op jit(solution)/shard_map/ppermute | solution.py:448
  36.1 0.9 %copy-start.11 = (f32[2,128,128]{2,1,0:T(8,128)S(1)}, f32[2,128,128]{2,1,0:T(8,128)}, u32[]{:S(2)}) copy-start(f32[2,128,128]{2,1,0:T(8,128)} %get-tuple-element.32.taps) | copy-start | bytes 393220
  37.0 6.5 %copy-start.8 = (s32[32]{0:T(128)S(1)}, s32[32]{0:T(128)}, u32[]{:S(2)}) copy-start(s32[32]{0:T(128)} %owners.3) | copy-start | bytes 388
  37.0 13.2 %copy-start.1 = (bf16[256,2048]{1,0:T(8,128)(2,1)S(1)}, bf16[256,2048]{1,0:T(8,128)(2,1)}, u32[]{:S(2)}) copy-start(bf16[256,2048]{1,0:T(8,128)(2,1)} %query.1) | copy-start | bytes 3145732
  42.5 1.0 %copy-start.2 = (bf16[256,2048]{1,0:T(8,128)(2,1)}, bf16[256,2048]{1,0:T(8,128)(2,1)S(1)}, u32[]{:S(2)}) copy-start(bf16[256,2048]{1,0:T(8,128)(2,1)S(1)} %get-tuple-element.43.weight) | copy-start | bytes 3145732
  43.4 6.8 %copy-start = (bf16[256,2048]{1,0:T(8,128)(2,1)}, bf16[256,2048]{1,0:T(8,128)(2,1)S(1)}, u32[]{:S(2)}) copy-start(bf16[256,2048]{1,0:T(8,128)(2,1)S(1)} %get-tuple-element.33.rest_9_.local) | copy-start | bytes 3145732
  45.8 7.2 %collective-permute-start.10 = (bf16[1,16,2048]{2,1,0:T(8,128)(2,1)S(1)}, bf16[1,16,2048]{2,1,0:T(8,128)(2,1)S(1)}, u32[]{:S(2)}, u32[]{:S(2)}) collective-permute-start(bf16[1,16,2048]{2,1,0:T(8,128)(2,1)S(1)} %get-tuple-element.47), channel_id=1, source_target_pairs={{0,3},{1,2},{2,1},{3,0},{4,7},{5,6},{6,5},{7,4},{8,11},{9,10},{10,... | collective-permute-start | bytes 196616 | tf_op jit(solution)/shard_map/ppermute | solution.py:496
  49.4 5.9 %collective-permute-start.8 = (bf16[1,16,2048]{2,1,0:T(8,128)(2,1)S(1)}, bf16[1,16,2048]{2,1,0:T(8,128)(2,1)S(1)}, u32[]{:S(2)}, u32[]{:S(2)}) collective-permute-start(bf16[1,16,2048]{2,1,0:T(8,128)(2,1)S(1)} %get-tuple-element.45), channel_id=1, source_target_pairs={{0,1},{1,0},{2,3},{3,2},{4,5},{5,4},{6,7},{7,6},{8,9},{9,8},{10,11... | collective-permute-start | bytes 196616 | tf_op jit(solution)/shard_map/ppermute | solution.py:496
  49.4 6.9 %collective-permute-start.9 = (bf16[1,16,2048]{2,1,0:T(8,128)(2,1)S(1)}, bf16[1,16,2048]{2,1,0:T(8,128)(2,1)S(1)}, u32[]{:S(2)}, u32[]{:S(2)}) collective-permute-start(bf16[1,16,2048]{2,1,0:T(8,128)(2,1)S(1)} %get-tuple-element.46), channel_id=1, source_target_pairs={{0,2},{1,3},{2,0},{3,1},{4,6},{5,7},{6,4},{7,5},{8,10},{9,11},{10,... | collective-permute-start | bytes 196616 | tf_op jit(solution)/shard_map/ppermute | solution.py:496

commit v3 on v2

--- a/solution.py
+++ b/solution.py
@@ -12,7 +12,7 @@
 LANES = 128
 BLOCK = 1024
 PART = 512
-CHUNK = 16
+CHUNK = 32
 F32 = jnp.float32
 BF16 = jnp.bfloat16
 

time: 57.5 us -> 57.3 us (level)
  no operation moved by 1% of the time
where the time goes in v3:
time: 57.3 us; the launch traced here: 57 us
  Pallas kernels  28.9 us (50%)
  starting transfers between devices  19.6 us (34%)
  waiting for transfers between devices  4.21 us (7%)
  local copies, waits for them, and re-layouts  3.37 us (6%)
  between operations  0.85 us (1%)
    ppermute x7, starting transfers between devices, per_device(): got.append(lax.ppermute(ends[d], 'ctx', route))  12.8 us
    pallas_call x1, Pallas kernels, per_device(): pl.pallas_call(functools.partial(states_kernel, cap, size), grid=(width /...  8.8 us
    pallas_call x1, Pallas kernels, per_device(): pl.pallas_call(functools.partial(second_kernel, size), grid=(width // blo...  5.47 us
    pallas_call x1, Pallas kernels, per_device(): pl.pallas_call(functools.partial(local_kernel, size), grid=(width // broa...  5.46 us
    ppermute x3, starting transfers between devices, per_device(): arrived.append(lax.ppermute(picked[d], 'ch', route))  4.45 us
    ppermute x3, waiting for transfers between devices, per_device(): arrived.append(lax.ppermute(picked[d], 'ch', route))  3.36 us
    pallas_call x1, Pallas kernels, per_device(): pl.pallas_call(functools.partial(prepare_kernel, cap, peers, size), in_sp...  3.34 us
    pallas_call x1, Pallas kernels, per_device(): pl.pallas_call(functools.partial(output_kernel, size), grid=(width // thi...  2.75 us
  transfers between devices with their start and end apart: 11, of which 3 were waited for; matrix products, arithmetic and copies ran while one was open for 1% of the time, Pallas kernels for 30%

profile of v3, /device:TPU:0, one launch (start us, length us, event | category | flops | bytes accessed | tf_op | source)
XLA Modules:
  0.0 57.0 jit_solution(963587195963921815)
XLA Ops:
  0.6 1.1 %slice.3 = bf16[128,2048]{1,0:T(8,128)(2,1)S(1)} slice(bf16[256,2048]{1,0:T(8,128)(2,1)} %value.3), slice={[128:256], [0:2048]} | slice | bytes 1048576 | tf_op jit(solution)/shard_map/slice | solution.py:366
  1.7 2.4 %collective-permute-start = (bf16[128,2048]{1,0:T(8,128)(2,1)S(1)}, bf16[128,2048]{1,0:T(8,128)(2,1)S(1)}, u32[]{:S(2)}, u32[]{:S(2)}) collective-permute-start(bf16[128,2048]{1,0:T(8,128)(2,1)S(1)} %slice.3), channel_id=1, source_target_pairs={{0,4},{4,8},{8,12},{12,16},{16,20},{20,24},{24,28},{1,5},{5,9},{9,... | collective-permute-start | bytes 1572872 | tf_op jit(solution)/shard_map/ppermute | solution.py:365
  4.1 3.3 %prepare.1 = (f32[16,2048]{1,0:T(8,128)}, f32[16,2048]{1,0:T(8,128)}, f32[128,128]{1,0:T(8,128)}, bf16[5,128,128]{2,1,0:T(8,128)(2,1)}, f32[2,128,128]{2,1,0:T(8,128)}, /*index=5*/f32[256]{0:T(256)}, s32[16]{0:T(128)}) custom-call(s32[65]{0:T(128)} %offsets.5, s32[32]{0:T(128)} %owners.3, s32[1]{0:T(128)} %bitcast.place, bf16[128,128]{1,0:T(8,128)(2,1)} %filt.1, ...), custom_call_target="tpu_custom_call" | custom-call | flops 1073741824 | bytes 1048576 | tf_op jit(solution)/shard_map/prepare/pallas_call | solution.py:379
  7.5 0.0 copy-start.3
  7.5 0.0 copy-start.4
  7.5 0.0 copy-start.5
  7.5 0.0 copy-start.6
  7.5 0.0 copy-start.9
  7.5 5.5 %second.1.kept = bf16[144,128,128]{2,1,0:T(8,128)(2,1)} custom-call(bf16[256,2048]{1,0:T(8,128)(2,1)} %value.3, bf16[256,2048]{1,0:T(8,128)(2,1)} %key.3, f32[128,128]{1,0:T(8,128)} %get-tuple-element.27.rows, bf16[5,128,128]{2,1,0:T(8,128)(2,1)} %get-tuple-element.28.masks), custom_call_target="tpu_custom_call" | custom-call | flops 2147483648 | bytes 3670016 | tf_op jit(solution)/shard_map/second/pallas_call | solution.py:401
  13.0 0.0 copy-start.10
  13.0 0.0 collective-permute-done.halo
  13.0 0.0 copy-done.3
  13.0 0.0 copy-done.4
  13.0 0.0 copy-done.5
  13.1 0.0 copy-done.6
  13.1 8.8 %states.1 = (bf16[256,2048]{1,0:T(8,128)(2,1)S(1)}, bf16[3,16,2048]{2,1,0:T(8,128)(2,1)S(1)}, bf16[3,16,2048]{2,1,0:T(8,128)(2,1)S(1)}, bf16[3,16,2048]{2,1,0:T(...) custom-call(s32[1]{0:T(128)} %bitcast.place, ...), custom_call_target="tpu_custom_call" | custom-call | tf_op jit(solution)/shard_map/states/pallas_call | solution.py:419
  21.9 2.6 %collective-permute-start.1 = (bf16[3,16,2048]{2,1,0:T(8,128)(2,1)S(1)}, bf16[3,16,2048]{2,1,0:T(8,128)(2,1)S(1)}, u32[]{:S(2)}, u32[]{:S(2)}) collective-permute-start(bf16[3,16,2048]{2,1,0:T(8,128)(2,1)S(1)} %get-tuple-element.35), channel_id=1, source_target_pairs={{0,4},{4,8},{8,12},{12,16},{16,20},{20,24},{24,28},{28,0},{1,5},{5... | collective-permute-start | bytes 589832 | tf_op jit(solution)/shard_map/ppermute | solution.py:448
  24.5 1.5 %collective-permute-start.2 = (bf16[3,16,2048]{2,1,0:T(8,128)(2,1)S(1)}, bf16[3,16,2048]{2,1,0:T(8,128)(2,1)S(1)}, u32[]{:S(2)}, u32[]{:S(2)}) collective-permute-start(bf16[3,16,2048]{2,1,0:T(8,128)(2,1)S(1)} %get-tuple-element.36), channel_id=1, source_target_pairs={{0,8},{4,12},{8,16},{12,20},{16,24},{20,28},{24,0},{28,4},{1,9},{5... | collective-permute-start | bytes 589832 | tf_op jit(solution)/shard_map/ppermute | solution.py:448
  26.0 0.1 copy.13
  26.1 0.1 reshape.21.rates
  26.2 0.1 copy.14
  26.3 0.1 reshape.22.resid
  26.4 0.9 %collective-permute-start.3 = (bf16[3,16,2048]{2,1,0:T(8,128)(2,1)S(1)}, bf16[3,16,2048]{2,1,0:T(8,128)(2,1)S(1)}, u32[]{:S(2)}, u32[]{:S(2)}) collective-permute-start(bf16[3,16,2048]{2,1,0:T(8,128)(2,1)S(1)} %get-tuple-element.37), channel_id=1, source_target_pairs={{0,12},{4,16},{8,20},{12,24},{16,28},{20,0},{24,4},{28,8},{1,13},{... | collective-permute-start | bytes 589832 | tf_op jit(solution)/shard_map/ppermute | solution.py:448
  27.3 0.5 collective-permute-start.4
  27.8 0.4 collective-permute-start.5
  28.3 0.0 collective-permute-done.1.rest_1_
  28.3 3.7 %collective-permute-start.6 = (bf16[3,16,2048]{2,1,0:T(8,128)(2,1)S(1)}, bf16[3,16,2048]{2,1,0:T(8,128)(2,1)S(1)}, u32[]{:S(2)}, u32[]{:S(2)}) collective-permute-start(bf16[3,16,2048]{2,1,0:T(8,128)(2,1)S(1)} %get-tuple-element.40), channel_id=1, source_target_pairs={{0,24},{4,28},{8,0},{12,4},{16,8},{20,12},{24,16},{28,20},{1,25},{... | collective-permute-start | bytes 589832 | tf_op jit(solution)/shard_map/ppermute | solution.py:448
  32.0 0.8 %collective-permute-done.2.rest_2_ = bf16[3,16,2048]{2,1,0:T(8,128)(2,1)S(1)} collective-permute-done((bf16[3,16,2048]{2,1,0:T(8,128)(2,1)S(1)}, bf16[3,16,2048]{2,1,0:T(8,128)(2,1)S(1)}, u32[]{:S(2)}, u32[]{:S(2)}) %collective-permute-start.2) | collective-permute-done | bytes 196640 | tf_op jit(solution)/shard_map/ppermute | solution.py:448
  32.8 3.1 %collective-permute-start.7 = (bf16[3,16,2048]{2,1,0:T(8,128)(2,1)S(1)}, bf16[3,16,2048]{2,1,0:T(8,128)(2,1)S(1)}, u32[]{:S(2)}, u32[]{:S(2)}) collective-permute-start(bf16[3,16,2048]{2,1,0:T(8,128)(2,1)S(1)} %get-tuple-element.41), channel_id=1, source_target_pairs={{0,28},{4,0},{8,4},{12,8},{16,12},{20,16},{24,20},{28,24},{1,29},{... | collective-permute-start | bytes 589832 | tf_op jit(solution)/shard_map/ppermute | solution.py:448
  35.9 0.9 %copy-done.11 = f32[2,128,128]{2,1,0:T(8,128)S(1)} copy-done((f32[2,128,128]{2,1,0:T(8,128)S(1)}, f32[2,128,128]{2,1,0:T(8,128)}, u32[]{:S(2)}) %copy-start.11) | copy-done | bytes 131096
  36.8 5.5 %local.1 = (bf16[256,2048]{1,0:T(8,128)(2,1)S(1)}, bf16[256,2048]{1,0:T(8,128)(2,1)S(1)}) custom-call(s32[65]{0:T(128)S(1)} %copy-done.7, s32[1]{0:T(128)} %bitcast.place, bf16[256,2048]{1,0:T(8,128)(2,1)S(1)} %get-tuple-element.31.mixed, bf16[5,128,128]{2,1,0:T(8,128)(2,1)S(1)} %copy-done.4, f32[2,128,128]{2,1,0:T(8,128)S(1)} %copy-done.11, ...), custom_call_target="tpu_custom_call" | custom-call | flops 4294967296 | bytes 3145728 | tf_op jit(solution)/shard_map/local/pallas_call | solution.py:451
  42.3 0.0 copy-start.2
  42.3 0.9 %copy-done.2 = bf16[256,2048]{1,0:T(8,128)(2,1)} copy-done((bf16[256,2048]{1,0:T(8,128)(2,1)}, bf16[256,2048]{1,0:T(8,128)(2,1)S(1)}, u32[]{:S(2)}) %copy-start.2) | copy-done | bytes 1048600
  43.2 0.0 collective-permute-done.3.rest_3_
  43.3 0.0 collective-permute-done.4.rest_4_
  43.3 0.0 collective-permute-done.5.rest_5_
  43.3 0.0 collective-permute-done.6.rest_6_
  43.3 0.0 collective-permute-done.7.rest_7_
  43.3 2.3 %slots.1 = (f32[16,2048]{1,0:T(8,128)S(1)}, bf16[1,16,2048]{2,1,0:T(8,128)(2,1)S(1)}, bf16[1,16,2048]{2,1,0:T(8,128)(2,1)S(1)}, bf16[1,16,2048]{2,1,0:T(8,128)(2,1)S(1)}, bf16[1,16,2048]{2,1,0:T(8,128)(2,1)S(1)}) custom-call(s32[65]{0:T(128)S(1)} %copy-done.7, s32[32]{0:T(128)S(1)} %copy-done.8, s32[1]{0:T(128)} %bitcast.place, s32[1]{0:T(128)} %bitcast.4.line, ...), custom_call_target="tpu_custom_call" | custom-call | tf_op jit(solution)/shard_map/slots/pallas_call | solution.py:478
  45.6 3.6 %collective-permute-start.10 = (bf16[1,16,2048]{2,1,0:T(8,128)(2,1)S(1)}, bf16[1,16,2048]{2,1,0:T(8,128)(2,1)S(1)}, u32[]{:S(2)}, u32[]{:S(2)}) collective-permute-start(bf16[1,16,2048]{2,1,0:T(8,128)(2,1)S(1)} %get-tuple-element.47), channel_id=1, source_target_pairs={{0,3},{1,2},{2,1},{3,0},{4,7},{5,6},{6,5},{7,4},{8,11},{9,10},{10,... | collective-permute-start | bytes 196616 | tf_op jit(solution)/shard_map/ppermute | solution.py:496
  49.2 0.0 collective-permute-start.8
  49.2 0.8 %collective-permute-start.9 = (bf16[1,16,2048]{2,1,0:T(8,128)(2,1)S(1)}, bf16[1,16,2048]{2,1,0:T(8,128)(2,1)S(1)}, u32[]{:S(2)}, u32[]{:S(2)}) collective-permute-start(bf16[1,16,2048]{2,1,0:T(8,128)(2,1)S(1)} %get-tuple-element.46), channel_id=1, source_target_pairs={{0,2},{1,3},{2,0},{3,1},{4,6},{5,7},{6,4},{7,5},{8,10},{9,11},{10,... | collective-permute-start | bytes 196616 | tf_op jit(solution)/shard_map/ppermute | solution.py:496
  50.0 0.0 copy-done.1
  50.0 2.7 %output.1 = bf16[256,2048]{1,0:T(8,128)(2,1)} custom-call(bf16[256,2048]{1,0:T(8,128)(2,1)S(1)} %copy-done.1, bf16[256,2048]{1,0:T(8,128)(2,1)} %copy-done, f32[16,2048]{1,0:T(8,128)S(1)} %get-tuple-element.42.entering, bf16[256,2048]{1,0:T(8,128)(2,1)} %copy-done.2), custom_call_target="tpu_custom_call" | custom-call | flops 805306368 | bytes 6291456 | tf_op jit(solution)/shard_map/output/pallas_call | solution.py:499
  52.8 0.0 collective-permute-done.10.refs_3_
  52.8 2.3 %collective-permute-done.8.refs_1_ = bf16[1,16,2048]{2,1,0:T(8,128)(2,1)S(1)} collective-permute-done((bf16[1,16,2048]{2,1,0:T(8,128)(2,1)S(1)}, bf16[1,16,2048]{2,1,0:T(8,128)(2,1)S(1)}, u32[]{:S(2)}, u32[]{:S(2)}) %collective-permute-start.8) | collective-permute-done | bytes 65568 | tf_op jit(solution)/shard_map/ppermute | solution.py:496
  55.1 1.1 %collective-permute-done.9.refs_2_ = bf16[1,16,2048]{2,1,0:T(8,128)(2,1)S(1)} collective-permute-done((bf16[1,16,2048]{2,1,0:T(8,128)(2,1)S(1)}, bf16[1,16,2048]{2,1,0:T(8,128)(2,1)S(1)}, u32[]{:S(2)}, u32[]{:S(2)}) %collective-permute-start.9) | collective-permute-done | bytes 65568 | tf_op jit(solution)/shard_map/ppermute | solution.py:496
  56.1 0.8 %widen.1 = f32[1,16,8192]{2,1,0:T(8,128)} custom-call(s32[1]{0:T(128)} %bitcast.4.line, bf16[1,16,2048]{2,1,0:T(8,128)(2,1)S(1)} %get-tuple-element.44.refs_0_, bf16[1,16,2048]{2,1,0:T(8,128)(2,1)S(1)} %collective-permute-done.8.refs_1_, bf16[1,16,2048]{2,1,0:T(8,128)(2,1)S(1)} %collective-permute-done.9.refs_2_, ...), custom_call_target="tpu_custom_call" | custom-call | tf_op jit(solution)/shard_map/widen/pallas_call | solution.py:512
  (14 shorter events, 0.0 us)
Async XLA Ops:
  1.7 11.3 %collective-permute-start = (bf16[128,2048]{1,0:T(8,128)(2,1)S(1)}, bf16[128,2048]{1,0:T(8,128)(2,1)S(1)}, u32[]{:S(2)}, u32[]{:S(2)}) collective-permute-start(bf16[128,2048]{1,0:T(8,128)(2,1)S(1)} %slice.3), channel_id=1, source_target_pairs={{0,4},{4,8},{8,12},{12,16},{16,20},{20,24},{24,28},{1,5},{5,9},{9,... | collective-permute-start | bytes 1572872 | tf_op jit(solution)/shard_map/ppermute | solution.py:365
  7.5 5.6 %copy-start.3 = (f32[16,2048]{1,0:T(8,128)S(1)}, f32[16,2048]{1,0:T(8,128)}, u32[]{:S(2)}) copy-start(f32[16,2048]{1,0:T(8,128)} %get-tuple-element.29.rates.rest_8_) | copy-start | bytes 393220
  7.5 5.6 %copy-start.4 = (bf16[5,128,128]{2,1,0:T(8,128)(2,1)S(1)}, bf16[5,128,128]{2,1,0:T(8,128)(2,1)}, u32[]{:S(2)}) copy-start(bf16[5,128,128]{2,1,0:T(8,128)(2,1)} %get-tuple-element.28.masks) | copy-start | bytes 491524
  7.5 5.6 %copy-start.5 = (f32[16,2048]{1,0:T(8,128)S(1)}, f32[16,2048]{1,0:T(8,128)}, u32[]{:S(2)}) copy-start(f32[16,2048]{1,0:T(8,128)} %get-tuple-element.30.gains) | copy-start | bytes 393220
  7.5 5.6 %copy-start.6 = (f32[256]{0:T(256)S(1)}, f32[256]{0:T(256)}, u32[]{:S(2)}) copy-start(f32[256]{0:T(256)} %get-tuple-element.25.keep) | copy-start | bytes 3076
  7.5 5.6 %copy-start.9 = (s32[16]{0:T(128)S(1)}, s32[16]{0:T(128)}, u32[]{:S(2)}) copy-start(s32[16]{0:T(128)} %get-tuple-element.26.last) | copy-start | bytes 196
  13.0 13.0 %copy-start.12 = (f32[16,128]{1,0:T(8,128)S(1)}, f32[16,128]{1,0:T(8,128)}, u32[]{:S(2)}) copy-start(f32[16,128]{1,0:T(8,128)} %rates.1) | copy-start | bytes 24580
  13.0 13.2 %copy-start.13 = (f32[16,128]{1,0:T(8,128)S(1)}, f32[16,128]{1,0:T(8,128)}, u32[]{:S(2)}) copy-start(f32[16,128]{1,0:T(8,128)} %resid.1) | copy-start | bytes 24580
  13.0 22.9 %copy-start.7 = (s32[65]{0:T(128)S(1)}, s32[65]{0:T(128)}, u32[]{:S(2)}) copy-start(s32[65]{0:T(128)} %offsets.5) | copy-start | bytes 784
  13.0 22.9 %copy-start.10 = (f32[2048]{0:T(1024)S(1)}, f32[2048]{0:T(1024)}, u32[]{:S(2)}) copy-start(f32[2048]{0:T(1024)} %param.15) | copy-start | bytes 24580
  21.9 6.4 %collective-permute-start.1 = (bf16[3,16,2048]{2,1,0:T(8,128)(2,1)S(1)}, bf16[3,16,2048]{2,1,0:T(8,128)(2,1)S(1)}, u32[]{:S(2)}, u32[]{:S(2)}) collective-permute-start(bf16[3,16,2048]{2,1,0:T(8,128)(2,1)S(1)} %get-tuple-element.35), channel_id=1, source_target_pairs={{0,4},{4,8},{8,12},{12,16},{16,20},{20,24},{24,28},{28,0},{1,5},{5... | collective-permute-start | bytes 589832 | tf_op jit(solution)/shard_map/ppermute | solution.py:448
  24.5 8.3 %collective-permute-start.2 = (bf16[3,16,2048]{2,1,0:T(8,128)(2,1)S(1)}, bf16[3,16,2048]{2,1,0:T(8,128)(2,1)S(1)}, u32[]{:S(2)}, u32[]{:S(2)}) collective-permute-start(bf16[3,16,2048]{2,1,0:T(8,128)(2,1)S(1)} %get-tuple-element.36), channel_id=1, source_target_pairs={{0,8},{4,12},{8,16},{12,20},{16,24},{20,28},{24,0},{28,4},{1,9},{5... | collective-permute-start | bytes 589832 | tf_op jit(solution)/shard_map/ppermute | solution.py:448
  26.4 16.8 %collective-permute-start.3 = (bf16[3,16,2048]{2,1,0:T(8,128)(2,1)S(1)}, bf16[3,16,2048]{2,1,0:T(8,128)(2,1)S(1)}, u32[]{:S(2)}, u32[]{:S(2)}) collective-permute-start(bf16[3,16,2048]{2,1,0:T(8,128)(2,1)S(1)} %get-tuple-element.37), channel_id=1, source_target_pairs={{0,12},{4,16},{8,20},{12,24},{16,28},{20,0},{24,4},{28,8},{1,13},{... | collective-permute-start | bytes 589832 | tf_op jit(solution)/shard_map/ppermute | solution.py:448
  27.3 15.9 %collective-permute-start.4 = (bf16[3,16,2048]{2,1,0:T(8,128)(2,1)S(1)}, bf16[3,16,2048]{2,1,0:T(8,128)(2,1)S(1)}, u32[]{:S(2)}, u32[]{:S(2)}) collective-permute-start(bf16[3,16,2048]{2,1,0:T(8,128)(2,1)S(1)} %get-tuple-element.38), channel_id=1, source_target_pairs={{0,16},{4,20},{8,24},{12,28},{16,0},{20,4},{24,8},{28,12},{1,17},{... | collective-permute-start | bytes 589832 | tf_op jit(solution)/shard_map/ppermute | solution.py:448
  27.8 15.4 %collective-permute-start.5 = (bf16[3,16,2048]{2,1,0:T(8,128)(2,1)S(1)}, bf16[3,16,2048]{2,1,0:T(8,128)(2,1)S(1)}, u32[]{:S(2)}, u32[]{:S(2)}) collective-permute-start(bf16[3,16,2048]{2,1,0:T(8,128)(2,1)S(1)} %get-tuple-element.39), channel_id=1, source_target_pairs={{0,20},{4,24},{8,28},{12,0},{16,4},{20,8},{24,12},{28,16},{1,21},{... | collective-permute-start | bytes 589832 | tf_op jit(solution)/shard_map/ppermute | solution.py:448
  28.3 15.0 %collective-permute-start.6 = (bf16[3,16,2048]{2,1,0:T(8,128)(2,1)S(1)}, bf16[3,16,2048]{2,1,0:T(8,128)(2,1)S(1)}, u32[]{:S(2)}, u32[]{:S(2)}) collective-permute-start(bf16[3,16,2048]{2,1,0:T(8,128)(2,1)S(1)} %get-tuple-element.40), channel_id=1, source_target_pairs={{0,24},{4,28},{8,0},{12,4},{16,8},{20,12},{24,16},{28,20},{1,25},{... | collective-permute-start | bytes 589832 | tf_op jit(solution)/shard_map/ppermute | solution.py:448
  32.8 10.5 %collective-permute-start.7 = (bf16[3,16,2048]{2,1,0:T(8,128)(2,1)S(1)}, bf16[3,16,2048]{2,1,0:T(8,128)(2,1)S(1)}, u32[]{:S(2)}, u32[]{:S(2)}) collective-permute-start(bf16[3,16,2048]{2,1,0:T(8,128)(2,1)S(1)} %get-tuple-element.41), channel_id=1, source_target_pairs={{0,28},{4,0},{8,4},{12,8},{16,12},{20,16},{24,20},{28,24},{1,29},{... | collective-permute-start | bytes 589832 | tf_op jit(solution)/shard_map/ppermute | solution.py:448
  35.9 0.9 %copy-start.11 = (f32[2,128,128]{2,1,0:T(8,128)S(1)}, f32[2,128,128]{2,1,0:T(8,128)}, u32[]{:S(2)}) copy-start(f32[2,128,128]{2,1,0:T(8,128)} %get-tuple-element.32.taps) | copy-start | bytes 393220
  36.8 6.5 %copy-start.8 = (s32[32]{0:T(128)S(1)}, s32[32]{0:T(128)}, u32[]{:S(2)}) copy-start(s32[32]{0:T(128)} %owners.3) | copy-start | bytes 388
  36.8 13.2 %copy-start.1 = (bf16[256,2048]{1,0:T(8,128)(2,1)S(1)}, bf16[256,2048]{1,0:T(8,128)(2,1)}, u32[]{:S(2)}) copy-start(bf16[256,2048]{1,0:T(8,128)(2,1)} %query.1) | copy-start | bytes 3145732
  42.3 1.0 %copy-start.2 = (bf16[256,2048]{1,0:T(8,128)(2,1)}, bf16[256,2048]{1,0:T(8,128)(2,1)S(1)}, u32[]{:S(2)}) copy-start(bf16[256,2048]{1,0:T(8,128)(2,1)S(1)} %get-tuple-element.43.weight) | copy-start | bytes 3145732
  43.2 6.8 %copy-start = (bf16[256,2048]{1,0:T(8,128)(2,1)}, bf16[256,2048]{1,0:T(8,128)(2,1)S(1)}, u32[]{:S(2)}) copy-start(bf16[256,2048]{1,0:T(8,128)(2,1)S(1)} %get-tuple-element.33.rest_9_.local) | copy-start | bytes 3145732
  45.6 7.2 %collective-permute-start.10 = (bf16[1,16,2048]{2,1,0:T(8,128)(2,1)S(1)}, bf16[1,16,2048]{2,1,0:T(8,128)(2,1)S(1)}, u32[]{:S(2)}, u32[]{:S(2)}) collective-permute-start(bf16[1,16,2048]{2,1,0:T(8,128)(2,1)S(1)} %get-tuple-element.47), channel_id=1, source_target_pairs={{0,3},{1,2},{2,1},{3,0},{4,7},{5,6},{6,5},{7,4},{8,11},{9,10},{10,... | collective-permute-start | bytes 196616 | tf_op jit(solution)/shard_map/ppermute | solution.py:496
  49.2 5.9 %collective-permute-start.8 = (bf16[1,16,2048]{2,1,0:T(8,128)(2,1)S(1)}, bf16[1,16,2048]{2,1,0:T(8,128)(2,1)S(1)}, u32[]{:S(2)}, u32[]{:S(2)}) collective-permute-start(bf16[1,16,2048]{2,1,0:T(8,128)(2,1)S(1)} %get-tuple-element.45), channel_id=1, source_target_pairs={{0,1},{1,0},{2,3},{3,2},{4,5},{5,4},{6,7},{7,6},{8,9},{9,8},{10,11... | collective-permute-start | bytes 196616 | tf_op jit(solution)/shard_map/ppermute | solution.py:496
  49.2 6.9 %collective-permute-start.9 = (bf16[1,16,2048]{2,1,0:T(8,128)(2,1)S(1)}, bf16[1,16,2048]{2,1,0:T(8,128)(2,1)S(1)}, u32[]{:S(2)}, u32[]{:S(2)}) collective-permute-start(bf16[1,16,2048]{2,1,0:T(8,128)(2,1)S(1)} %get-tuple-element.46), channel_id=1, source_target_pairs={{0,2},{1,3},{2,0},{3,1},{4,6},{5,7},{6,4},{7,5},{8,10},{9,11},{10,... | collective-permute-start | bytes 196616 | tf_op jit(solution)/shard_map/ppermute | solution.py:496

commit v4 on v3

--- a/solution.py
+++ b/solution.py
@@ -12,7 +12,7 @@
 LANES = 128
 BLOCK = 1024
 PART = 512
-CHUNK = 32
+CHUNK = 64
 F32 = jnp.float32
 BF16 = jnp.bfloat16
 

time: 57.3 us -> 57.2 us (level)
  no operation moved by 1% of the time
where the time goes in v4:
time: 57.2 us; the launch traced here: 56.9 us
  Pallas kernels  28.8 us (50%)
  starting transfers between devices  19.6 us (34%)
  waiting for transfers between devices  4.21 us (7%)
  local copies, waits for them, and re-layouts  3.37 us (6%)
  between operations  0.85 us (1%)
    ppermute x7, starting transfers between devices, per_device(): got.append(lax.ppermute(ends[d], 'ctx', route))  12.8 us
    pallas_call x1, Pallas kernels, per_device(): pl.pallas_call(functools.partial(states_kernel, cap, size), grid=(width /...  8.7 us
    pallas_call x1, Pallas kernels, per_device(): pl.pallas_call(functools.partial(second_kernel, size), grid=(width // blo...  5.47 us
    pallas_call x1, Pallas kernels, per_device(): pl.pallas_call(functools.partial(local_kernel, size), grid=(width // broa...  5.46 us
    ppermute x3, starting transfers between devices, per_device(): arrived.append(lax.ppermute(picked[d], 'ch', route))  4.45 us
    ppermute x3, waiting for transfers between devices, per_device(): arrived.append(lax.ppermute(picked[d], 'ch', route))  3.36 us
    pallas_call x1, Pallas kernels, per_device(): pl.pallas_call(functools.partial(prepare_kernel, cap, peers, size), in_sp...  3.34 us
    pallas_call x1, Pallas kernels, per_device(): pl.pallas_call(functools.partial(output_kernel, size), grid=(width // thi...  2.75 us
  transfers between devices with their start and end apart: 11, of which 3 were waited for; matrix products, arithmetic and copies ran while one was open for 1% of the time, Pallas kernels for 30%

profile of v4, /device:TPU:0, one launch (start us, length us, event | category | flops | bytes accessed | tf_op | source)
XLA Modules:
  0.0 56.9 jit_solution(1342092413069924919)
XLA Ops:
  0.6 1.1 %slice.3 = bf16[128,2048]{1,0:T(8,128)(2,1)S(1)} slice(bf16[256,2048]{1,0:T(8,128)(2,1)} %value.3), slice={[128:256], [0:2048]} | slice | bytes 1048576 | tf_op jit(solution)/shard_map/slice | solution.py:366
  1.7 2.4 %collective-permute-start = (bf16[128,2048]{1,0:T(8,128)(2,1)S(1)}, bf16[128,2048]{1,0:T(8,128)(2,1)S(1)}, u32[]{:S(2)}, u32[]{:S(2)}) collective-permute-start(bf16[128,2048]{1,0:T(8,128)(2,1)S(1)} %slice.3), channel_id=1, source_target_pairs={{0,4},{4,8},{8,12},{12,16},{16,20},{20,24},{24,28},{1,5},{5,9},{9,... | collective-permute-start | bytes 1572872 | tf_op jit(solution)/shard_map/ppermute | solution.py:365
  4.1 3.3 %prepare.1 = (f32[16,2048]{1,0:T(8,128)}, f32[16,2048]{1,0:T(8,128)}, f32[128,128]{1,0:T(8,128)}, bf16[5,128,128]{2,1,0:T(8,128)(2,1)}, f32[2,128,128]{2,1,0:T(8,128)}, /*index=5*/f32[256]{0:T(256)}, s32[16]{0:T(128)}) custom-call(s32[65]{0:T(128)} %offsets.5, s32[32]{0:T(128)} %owners.3, s32[1]{0:T(128)} %bitcast.place, bf16[128,128]{1,0:T(8,128)(2,1)} %filt.1, ...), custom_call_target="tpu_custom_call" | custom-call | flops 1073741824 | bytes 1048576 | tf_op jit(solution)/shard_map/prepare/pallas_call | solution.py:379
  7.5 0.0 copy-start.3
  7.5 0.0 copy-start.4
  7.5 0.0 copy-start.5
  7.5 0.0 copy-start.6
  7.5 5.5 %second.1.kept = bf16[144,128,128]{2,1,0:T(8,128)(2,1)} custom-call(bf16[256,2048]{1,0:T(8,128)(2,1)} %value.3, bf16[256,2048]{1,0:T(8,128)(2,1)} %key.3, f32[128,128]{1,0:T(8,128)} %get-tuple-element.27.rows, bf16[5,128,128]{2,1,0:T(8,128)(2,1)} %get-tuple-element.28.masks), custom_call_target="tpu_custom_call" | custom-call | flops 2147483648 | bytes 3670016 | tf_op jit(solution)/shard_map/second/pallas_call | solution.py:401
  13.0 0.0 copy-start.10
  13.0 0.0 collective-permute-done.halo
  13.0 0.0 copy-done.3
  13.0 0.0 copy-done.4
  13.0 0.0 copy-done.5
  13.1 0.0 copy-done.6
  13.1 0.0 copy-done.9
  13.1 8.7 %states.1 = (bf16[256,2048]{1,0:T(8,128)(2,1)S(1)}, bf16[3,16,2048]{2,1,0:T(8,128)(2,1)S(1)}, bf16[3,16,2048]{2,1,0:T(8,128)(2,1)S(1)}, bf16[3,16,2048]{2,1,0:T(...) custom-call(s32[1]{0:T(128)} %bitcast.place, ...), custom_call_target="tpu_custom_call" | custom-call | tf_op jit(solution)/shard_map/states/pallas_call | solution.py:419
  21.8 2.6 %collective-permute-start.1 = (bf16[3,16,2048]{2,1,0:T(8,128)(2,1)S(1)}, bf16[3,16,2048]{2,1,0:T(8,128)(2,1)S(1)}, u32[]{:S(2)}, u32[]{:S(2)}) collective-permute-start(bf16[3,16,2048]{2,1,0:T(8,128)(2,1)S(1)} %get-tuple-element.35), channel_id=1, source_target_pairs={{0,4},{4,8},{8,12},{12,16},{16,20},{20,24},{24,28},{28,0},{1,5},{5... | collective-permute-start | bytes 589832 | tf_op jit(solution)/shard_map/ppermute | solution.py:448
  24.4 1.5 %collective-permute-start.2 = (bf16[3,16,2048]{2,1,0:T(8,128)(2,1)S(1)}, bf16[3,16,2048]{2,1,0:T(8,128)(2,1)S(1)}, u32[]{:S(2)}, u32[]{:S(2)}) collective-permute-start(bf16[3,16,2048]{2,1,0:T(8,128)(2,1)S(1)} %get-tuple-element.36), channel_id=1, source_target_pairs={{0,8},{4,12},{8,16},{12,20},{16,24},{20,28},{24,0},{28,4},{1,9},{5... | collective-permute-start | bytes 589832 | tf_op jit(solution)/shard_map/ppermute | solution.py:448
  25.9 0.1 copy.13
  26.0 0.1 reshape.21.rates
  26.1 0.0 copy-done.13
  26.1 0.1 copy.14
  26.2 0.1 reshape.22.resid
  26.3 0.9 %collective-permute-start.3 = (bf16[3,16,2048]{2,1,0:T(8,128)(2,1)S(1)}, bf16[3,16,2048]{2,1,0:T(8,128)(2,1)S(1)}, u32[]{:S(2)}, u32[]{:S(2)}) collective-permute-start(bf16[3,16,2048]{2,1,0:T(8,128)(2,1)S(1)} %get-tuple-element.37), channel_id=1, source_target_pairs={{0,12},{4,16},{8,20},{12,24},{16,28},{20,0},{24,4},{28,8},{1,13},{... | collective-permute-start | bytes 589832 | tf_op jit(solution)/shard_map/ppermute | solution.py:448
  27.2 0.5 collective-permute-start.4
  27.8 0.4 collective-permute-start.5
  28.2 0.0 collective-permute-done.1.rest_1_
  28.2 3.7 %collective-permute-start.6 = (bf16[3,16,2048]{2,1,0:T(8,128)(2,1)S(1)}, bf16[3,16,2048]{2,1,0:T(8,128)(2,1)S(1)}, u32[]{:S(2)}, u32[]{:S(2)}) collective-permute-start(bf16[3,16,2048]{2,1,0:T(8,128)(2,1)S(1)} %get-tuple-element.40), channel_id=1, source_target_pairs={{0,24},{4,28},{8,0},{12,4},{16,8},{20,12},{24,16},{28,20},{1,25},{... | collective-permute-start | bytes 589832 | tf_op jit(solution)/shard_map/ppermute | solution.py:448
  31.9 0.8 %collective-permute-done.2.rest_2_ = bf16[3,16,2048]{2,1,0:T(8,128)(2,1)S(1)} collective-permute-done((bf16[3,16,2048]{2,1,0:T(8,128)(2,1)S(1)}, bf16[3,16,2048]{2,1,0:T(8,128)(2,1)S(1)}, u32[]{:S(2)}, u32[]{:S(2)}) %collective-permute-start.2) | collective-permute-done | bytes 196640 | tf_op jit(solution)/shard_map/ppermute | solution.py:448
  32.7 3.1 %collective-permute-start.7 = (bf16[3,16,2048]{2,1,0:T(8,128)(2,1)S(1)}, bf16[3,16,2048]{2,1,0:T(8,128)(2,1)S(1)}, u32[]{:S(2)}, u32[]{:S(2)}) collective-permute-start(bf16[3,16,2048]{2,1,0:T(8,128)(2,1)S(1)} %get-tuple-element.41), channel_id=1, source_target_pairs={{0,28},{4,0},{8,4},{12,8},{16,12},{20,16},{24,20},{28,24},{1,29},{... | collective-permute-start | bytes 589832 | tf_op jit(solution)/shard_map/ppermute | solution.py:448
  35.8 0.9 %copy-done.11 = f32[2,128,128]{2,1,0:T(8,128)S(1)} copy-done((f32[2,128,128]{2,1,0:T(8,128)S(1)}, f32[2,128,128]{2,1,0:T(8,128)}, u32[]{:S(2)}) %copy-start.11) | copy-done | bytes 131096
  36.7 5.5 %local.1 = (bf16[256,2048]{1,0:T(8,128)(2,1)S(1)}, bf16[256,2048]{1,0:T(8,128)(2,1)S(1)}) custom-call(s32[65]{0:T(128)S(1)} %copy-done.7, s32[1]{0:T(128)} %bitcast.place, bf16[256,2048]{1,0:T(8,128)(2,1)S(1)} %get-tuple-element.31.mixed, bf16[5,128,128]{2,1,0:T(8,128)(2,1)S(1)} %copy-done.4, f32[2,128,128]{2,1,0:T(8,128)S(1)} %copy-done.11, ...), custom_call_target="tpu_custom_call" | custom-call | flops 4294967296 | bytes 3145728 | tf_op jit(solution)/shard_map/local/pallas_call | solution.py:451
  42.2 0.9 %copy-done.2 = bf16[256,2048]{1,0:T(8,128)(2,1)} copy-done((bf16[256,2048]{1,0:T(8,128)(2,1)}, bf16[256,2048]{1,0:T(8,128)(2,1)S(1)}, u32[]{:S(2)}) %copy-start.2) | copy-done | bytes 1048600
  43.2 0.0 collective-permute-done.3.rest_3_
  43.2 0.0 collective-permute-done.4.rest_4_
  43.2 0.0 collective-permute-done.5.rest_5_
  43.2 0.0 collective-permute-done.6.rest_6_
  43.2 0.0 collective-permute-done.7.rest_7_
  43.2 2.3 %slots.1 = (f32[16,2048]{1,0:T(8,128)S(1)}, bf16[1,16,2048]{2,1,0:T(8,128)(2,1)S(1)}, bf16[1,16,2048]{2,1,0:T(8,128)(2,1)S(1)}, bf16[1,16,2048]{2,1,0:T(8,128)(2,1)S(1)}, bf16[1,16,2048]{2,1,0:T(8,128)(2,1)S(1)}) custom-call(s32[65]{0:T(128)S(1)} %copy-done.7, s32[32]{0:T(128)S(1)} %copy-done.8, s32[1]{0:T(128)} %bitcast.place, s32[1]{0:T(128)} %bitcast.4.line, ...), custom_call_target="tpu_custom_call" | custom-call | tf_op jit(solution)/shard_map/slots/pallas_call | solution.py:478
  45.5 3.6 %collective-permute-start.10 = (bf16[1,16,2048]{2,1,0:T(8,128)(2,1)S(1)}, bf16[1,16,2048]{2,1,0:T(8,128)(2,1)S(1)}, u32[]{:S(2)}, u32[]{:S(2)}) collective-permute-start(bf16[1,16,2048]{2,1,0:T(8,128)(2,1)S(1)} %get-tuple-element.47), channel_id=1, source_target_pairs={{0,3},{1,2},{2,1},{3,0},{4,7},{5,6},{6,5},{7,4},{8,11},{9,10},{10,... | collective-permute-start | bytes 196616 | tf_op jit(solution)/shard_map/ppermute | solution.py:496
  49.1 0.0 collective-permute-start.8
  49.1 0.8 %collective-permute-start.9 = (bf16[1,16,2048]{2,1,0:T(8,128)(2,1)S(1)}, bf16[1,16,2048]{2,1,0:T(8,128)(2,1)S(1)}, u32[]{:S(2)}, u32[]{:S(2)}) collective-permute-start(bf16[1,16,2048]{2,1,0:T(8,128)(2,1)S(1)} %get-tuple-element.46), channel_id=1, source_target_pairs={{0,2},{1,3},{2,0},{3,1},{4,6},{5,7},{6,4},{7,5},{8,10},{9,11},{10,... | collective-permute-start | bytes 196616 | tf_op jit(solution)/shard_map/ppermute | solution.py:496
  49.9 0.0 copy-done
  49.9 2.7 %output.1 = bf16[256,2048]{1,0:T(8,128)(2,1)} custom-call(bf16[256,2048]{1,0:T(8,128)(2,1)S(1)} %copy-done.1, bf16[256,2048]{1,0:T(8,128)(2,1)} %copy-done, f32[16,2048]{1,0:T(8,128)S(1)} %get-tuple-element.42.entering, bf16[256,2048]{1,0:T(8,128)(2,1)} %copy-done.2), custom_call_target="tpu_custom_call" | custom-call | flops 805306368 | bytes 6291456 | tf_op jit(solution)/shard_map/output/pallas_call | solution.py:499
  52.7 0.0 collective-permute-done.10.refs_3_
  52.7 2.3 %collective-permute-done.8.refs_1_ = bf16[1,16,2048]{2,1,0:T(8,128)(2,1)S(1)} collective-permute-done((bf16[1,16,2048]{2,1,0:T(8,128)(2,1)S(1)}, bf16[1,16,2048]{2,1,0:T(8,128)(2,1)S(1)}, u32[]{:S(2)}, u32[]{:S(2)}) %collective-permute-start.8) | collective-permute-done | bytes 65568 | tf_op jit(solution)/shard_map/ppermute | solution.py:496
  55.0 1.1 %collective-permute-done.9.refs_2_ = bf16[1,16,2048]{2,1,0:T(8,128)(2,1)S(1)} collective-permute-done((bf16[1,16,2048]{2,1,0:T(8,128)(2,1)S(1)}, bf16[1,16,2048]{2,1,0:T(8,128)(2,1)S(1)}, u32[]{:S(2)}, u32[]{:S(2)}) %collective-permute-start.9) | collective-permute-done | bytes 65568 | tf_op jit(solution)/shard_map/ppermute | solution.py:496
  56.0 0.8 %widen.1 = f32[1,16,8192]{2,1,0:T(8,128)} custom-call(s32[1]{0:T(128)} %bitcast.4.line, bf16[1,16,2048]{2,1,0:T(8,128)(2,1)S(1)} %get-tuple-element.44.refs_0_, bf16[1,16,2048]{2,1,0:T(8,128)(2,1)S(1)} %collective-permute-done.8.refs_1_, bf16[1,16,2048]{2,1,0:T(8,128)(2,1)S(1)} %collective-permute-done.9.refs_2_, ...), custom_call_target="tpu_custom_call" | custom-call | tf_op jit(solution)/shard_map/widen/pallas_call | solution.py:512
  (14 shorter events, 0.0 us)
Async XLA Ops:
  1.7 11.3 %collective-permute-start = (bf16[128,2048]{1,0:T(8,128)(2,1)S(1)}, bf16[128,2048]{1,0:T(8,128)(2,1)S(1)}, u32[]{:S(2)}, u32[]{:S(2)}) collective-permute-start(bf16[128,2048]{1,0:T(8,128)(2,1)S(1)} %slice.3), channel_id=1, source_target_pairs={{0,4},{4,8},{8,12},{12,16},{16,20},{20,24},{24,28},{1,5},{5,9},{9,... | collective-permute-start | bytes 1572872 | tf_op jit(solution)/shard_map/ppermute | solution.py:365
  7.5 5.6 %copy-start.3 = (f32[16,2048]{1,0:T(8,128)S(1)}, f32[16,2048]{1,0:T(8,128)}, u32[]{:S(2)}) copy-start(f32[16,2048]{1,0:T(8,128)} %get-tuple-element.29.rates.rest_8_) | copy-start | bytes 393220
  7.5 5.6 %copy-start.4 = (bf16[5,128,128]{2,1,0:T(8,128)(2,1)S(1)}, bf16[5,128,128]{2,1,0:T(8,128)(2,1)}, u32[]{:S(2)}) copy-start(bf16[5,128,128]{2,1,0:T(8,128)(2,1)} %get-tuple-element.28.masks) | copy-start | bytes 491524
  7.5 5.6 %copy-start.5 = (f32[16,2048]{1,0:T(8,128)S(1)}, f32[16,2048]{1,0:T(8,128)}, u32[]{:S(2)}) copy-start(f32[16,2048]{1,0:T(8,128)} %get-tuple-element.30.gains) | copy-start | bytes 393220
  7.5 5.6 %copy-start.6 = (f32[256]{0:T(256)S(1)}, f32[256]{0:T(256)}, u32[]{:S(2)}) copy-start(f32[256]{0:T(256)} %get-tuple-element.25.keep) | copy-start | bytes 3076
  7.5 5.6 %copy-start.9 = (s32[16]{0:T(128)S(1)}, s32[16]{0:T(128)}, u32[]{:S(2)}) copy-start(s32[16]{0:T(128)} %get-tuple-element.26.last) | copy-start | bytes 196
  13.0 12.9 %copy-start.12 = (f32[16,128]{1,0:T(8,128)S(1)}, f32[16,128]{1,0:T(8,128)}, u32[]{:S(2)}) copy-start(f32[16,128]{1,0:T(8,128)} %rates.1) | copy-start | bytes 24580
  13.0 13.1 %copy-start.13 = (f32[16,128]{1,0:T(8,128)S(1)}, f32[16,128]{1,0:T(8,128)}, u32[]{:S(2)}) copy-start(f32[16,128]{1,0:T(8,128)} %resid.1) | copy-start | bytes 24580
  13.0 22.8 %copy-start.7 = (s32[65]{0:T(128)S(1)}, s32[65]{0:T(128)}, u32[]{:S(2)}) copy-start(s32[65]{0:T(128)} %offsets.5) | copy-start | bytes 784
  13.0 22.8 %copy-start.10 = (f32[2048]{0:T(1024)S(1)}, f32[2048]{0:T(1024)}, u32[]{:S(2)}) copy-start(f32[2048]{0:T(1024)} %param.15) | copy-start | bytes 24580
  21.8 6.4 %collective-permute-start.1 = (bf16[3,16,2048]{2,1,0:T(8,128)(2,1)S(1)}, bf16[3,16,2048]{2,1,0:T(8,128)(2,1)S(1)}, u32[]{:S(2)}, u32[]{:S(2)}) collective-permute-start(bf16[3,16,2048]{2,1,0:T(8,128)(2,1)S(1)} %get-tuple-element.35), channel_id=1, source_target_pairs={{0,4},{4,8},{8,12},{12,16},{16,20},{20,24},{24,28},{28,0},{1,5},{5... | collective-permute-start | bytes 589832 | tf_op jit(solution)/shard_map/ppermute | solution.py:448
  24.4 8.3 %collective-permute-start.2 = (bf16[3,16,2048]{2,1,0:T(8,128)(2,1)S(1)}, bf16[3,16,2048]{2,1,0:T(8,128)(2,1)S(1)}, u32[]{:S(2)}, u32[]{:S(2)}) collective-permute-start(bf16[3,16,2048]{2,1,0:T(8,128)(2,1)S(1)} %get-tuple-element.36), channel_id=1, source_target_pairs={{0,8},{4,12},{8,16},{12,20},{16,24},{20,28},{24,0},{28,4},{1,9},{5... | collective-permute-start | bytes 589832 | tf_op jit(solution)/shard_map/ppermute | solution.py:448
  26.3 16.8 %collective-permute-start.3 = (bf16[3,16,2048]{2,1,0:T(8,128)(2,1)S(1)}, bf16[3,16,2048]{2,1,0:T(8,128)(2,1)S(1)}, u32[]{:S(2)}, u32[]{:S(2)}) collective-permute-start(bf16[3,16,2048]{2,1,0:T(8,128)(2,1)S(1)} %get-tuple-element.37), channel_id=1, source_target_pairs={{0,12},{4,16},{8,20},{12,24},{16,28},{20,0},{24,4},{28,8},{1,13},{... | collective-permute-start | bytes 589832 | tf_op jit(solution)/shard_map/ppermute | solution.py:448
  27.2 15.9 %collective-permute-start.4 = (bf16[3,16,2048]{2,1,0:T(8,128)(2,1)S(1)}, bf16[3,16,2048]{2,1,0:T(8,128)(2,1)S(1)}, u32[]{:S(2)}, u32[]{:S(2)}) collective-permute-start(bf16[3,16,2048]{2,1,0:T(8,128)(2,1)S(1)} %get-tuple-element.38), channel_id=1, source_target_pairs={{0,16},{4,20},{8,24},{12,28},{16,0},{20,4},{24,8},{28,12},{1,17},{... | collective-permute-start | bytes 589832 | tf_op jit(solution)/shard_map/ppermute | solution.py:448
  27.8 15.4 %collective-permute-start.5 = (bf16[3,16,2048]{2,1,0:T(8,128)(2,1)S(1)}, bf16[3,16,2048]{2,1,0:T(8,128)(2,1)S(1)}, u32[]{:S(2)}, u32[]{:S(2)}) collective-permute-start(bf16[3,16,2048]{2,1,0:T(8,128)(2,1)S(1)} %get-tuple-element.39), channel_id=1, source_target_pairs={{0,20},{4,24},{8,28},{12,0},{16,4},{20,8},{24,12},{28,16},{1,21},{... | collective-permute-start | bytes 589832 | tf_op jit(solution)/shard_map/ppermute | solution.py:448
  28.2 15.0 %collective-permute-start.6 = (bf16[3,16,2048]{2,1,0:T(8,128)(2,1)S(1)}, bf16[3,16,2048]{2,1,0:T(8,128)(2,1)S(1)}, u32[]{:S(2)}, u32[]{:S(2)}) collective-permute-start(bf16[3,16,2048]{2,1,0:T(8,128)(2,1)S(1)} %get-tuple-element.40), channel_id=1, source_target_pairs={{0,24},{4,28},{8,0},{12,4},{16,8},{20,12},{24,16},{28,20},{1,25},{... | collective-permute-start | bytes 589832 | tf_op jit(solution)/shard_map/ppermute | solution.py:448
  32.7 10.5 %collective-permute-start.7 = (bf16[3,16,2048]{2,1,0:T(8,128)(2,1)S(1)}, bf16[3,16,2048]{2,1,0:T(8,128)(2,1)S(1)}, u32[]{:S(2)}, u32[]{:S(2)}) collective-permute-start(bf16[3,16,2048]{2,1,0:T(8,128)(2,1)S(1)} %get-tuple-element.41), channel_id=1, source_target_pairs={{0,28},{4,0},{8,4},{12,8},{16,12},{20,16},{24,20},{28,24},{1,29},{... | collective-permute-start | bytes 589832 | tf_op jit(solution)/shard_map/ppermute | solution.py:448
  35.8 0.9 %copy-start.11 = (f32[2,128,128]{2,1,0:T(8,128)S(1)}, f32[2,128,128]{2,1,0:T(8,128)}, u32[]{:S(2)}) copy-start(f32[2,128,128]{2,1,0:T(8,128)} %get-tuple-element.32.taps) | copy-start | bytes 393220
  36.7 6.5 %copy-start.8 = (s32[32]{0:T(128)S(1)}, s32[32]{0:T(128)}, u32[]{:S(2)}) copy-start(s32[32]{0:T(128)} %owners.3) | copy-start | bytes 388
  36.7 13.2 %copy-start.1 = (bf16[256,2048]{1,0:T(8,128)(2,1)S(1)}, bf16[256,2048]{1,0:T(8,128)(2,1)}, u32[]{:S(2)}) copy-start(bf16[256,2048]{1,0:T(8,128)(2,1)} %query.1) | copy-start | bytes 3145732
  42.2 1.0 %copy-start.2 = (bf16[256,2048]{1,0:T(8,128)(2,1)}, bf16[256,2048]{1,0:T(8,128)(2,1)S(1)}, u32[]{:S(2)}) copy-start(bf16[256,2048]{1,0:T(8,128)(2,1)S(1)} %get-tuple-element.43.weight) | copy-start | bytes 3145732
  43.2 6.8 %copy-start = (bf16[256,2048]{1,0:T(8,128)(2,1)}, bf16[256,2048]{1,0:T(8,128)(2,1)S(1)}, u32[]{:S(2)}) copy-start(bf16[256,2048]{1,0:T(8,128)(2,1)S(1)} %get-tuple-element.33.rest_9_.local) | copy-start | bytes 3145732
  45.5 7.2 %collective-permute-start.10 = (bf16[1,16,2048]{2,1,0:T(8,128)(2,1)S(1)}, bf16[1,16,2048]{2,1,0:T(8,128)(2,1)S(1)}, u32[]{:S(2)}, u32[]{:S(2)}) collective-permute-start(bf16[1,16,2048]{2,1,0:T(8,128)(2,1)S(1)} %get-tuple-element.47), channel_id=1, source_target_pairs={{0,3},{1,2},{2,1},{3,0},{4,7},{5,6},{6,5},{7,4},{8,11},{9,10},{10,... | collective-permute-start | bytes 196616 | tf_op jit(solution)/shard_map/ppermute | solution.py:496
  49.1 5.9 %collective-permute-start.8 = (bf16[1,16,2048]{2,1,0:T(8,128)(2,1)S(1)}, bf16[1,16,2048]{2,1,0:T(8,128)(2,1)S(1)}, u32[]{:S(2)}, u32[]{:S(2)}) collective-permute-start(bf16[1,16,2048]{2,1,0:T(8,128)(2,1)S(1)} %get-tuple-element.45), channel_id=1, source_target_pairs={{0,1},{1,0},{2,3},{3,2},{4,5},{5,4},{6,7},{7,6},{8,9},{9,8},{10,11... | collective-permute-start | bytes 196616 | tf_op jit(solution)/shard_map/ppermute | solution.py:496
  49.1 6.9 %collective-permute-start.9 = (bf16[1,16,2048]{2,1,0:T(8,128)(2,1)S(1)}, bf16[1,16,2048]{2,1,0:T(8,128)(2,1)S(1)}, u32[]{:S(2)}, u32[]{:S(2)}) collective-permute-start(bf16[1,16,2048]{2,1,0:T(8,128)(2,1)S(1)} %get-tuple-element.46), channel_id=1, source_target_pairs={{0,2},{1,3},{2,0},{3,1},{4,6},{5,7},{6,4},{7,5},{8,10},{9,11},{10,... | collective-permute-start | bytes 196616 | tf_op jit(solution)/shard_map/ppermute | solution.py:496
